TPU v7x, 128 devices: a whole 4x4x4 slice. The times are simulated.
128 devices in a mesh: replica: 16 (over z, x_hi, core), shard: 8 (over x_lo, y).
Axes of the slice: x: 4 (x_hi: 2, x_lo: 2; x = x_hi * 2 + x_lo), y: 4, z: 4, core: 2. Of those that a mesh axis runs over, the one named last changes fastest.
Arguments:
- tokens: bfloat16 [16384, 1024], P(('replica', 'shard')), may hold values from -6 to 6
- grad_out: bfloat16 [16384, 1024], P(('replica', 'shard')), may hold values from -6 to 6
- slope_index: int32 [16], replicated, may hold values from 0 to 15, each once
- ln1_gain: bfloat16 [2, 1024], P(None, 'shard'), may hold values from 0.5 to 1.5
- ln1_bias: bfloat16 [2, 1024], P(None, 'shard'), may hold values from -1 to 1
- qkv_weight: bfloat16 [2, 1024, 3072], P(None, 'shard'), may hold values from -0.1875 to 0.1875
- q_bias: bfloat16 [2, 1024], P(None, 'shard'), may hold values from -1 to 1
- v_bias: bfloat16 [2, 1024], P(None, 'shard'), may hold values from -1 to 1
- dense_weight: bfloat16 [2, 1024, 1024], P(None, 'shard'), may hold values from -0.375 to 0.375
- dense_bias: bfloat16 [2, 1024], P(None, 'shard'), may hold values from -1 to 1
- ln2_gain: bfloat16 [2, 1024], P(None, 'shard'), may hold values from 0.5 to 1.5
- ln2_bias: bfloat16 [2, 1024], P(None, 'shard'), may hold values from -1 to 1
- up_weight: bfloat16 [2, 1024, 4096], P(None, 'shard'), may hold values from -0.1875 to 0.1875
- up_bias: bfloat16 [2, 4096], P(None, 'shard'), may hold values from -1 to 1
- down_weight: bfloat16 [2, 4096, 1024], P(None, 'shard'), may hold values from -0.09375 to 0.09375
- down_bias: bfloat16 [2, 1024], P(None, 'shard'), may hold values from -1 to 1
Outputs:
- output: float32 [16384, 1024], P(('replica', 'shard'))
- grad_tokens: float32 [16384, 1024], P(('replica', 'shard'))
- grad_ln1_gain: float32 [2, 1024], P(None, 'shard')
- grad_ln1_bias: float32 [2, 1024], P(None, 'shard')
- grad_qkv_weight: float32 [2, 1024, 3072], P(None, 'shard')
- grad_q_bias: float32 [2, 1024], P(None, 'shard')
- grad_v_bias: float32 [2, 1024], P(None, 'shard')
- grad_dense_weight: float32 [2, 1024, 1024], P(None, 'shard')
- grad_dense_bias: float32 [2, 1024], P(None, 'shard')
- grad_ln2_gain: float32 [2, 1024], P(None, 'shard')
- grad_ln2_bias: float32 [2, 1024], P(None, 'shard')
- grad_up_weight: float32 [2, 1024, 4096], P(None, 'shard')
- grad_up_bias: float32 [2, 4096], P(None, 'shard')
- grad_down_weight: float32 [2, 4096, 1024], P(None, 'shard')
- grad_down_bias: float32 [2, 1024], P(None, 'shard')
Inputs may be any that keep to these rules, and one draw needn't show every extreme that they name: `slope_index`: each head has its own slope number, every number once.
All inputs are finite; a program needn't handle non-finite values.
Results may differ from a plain program's by a relative error of at most 0.025.
Values may be sent and summed in bfloat16 or wider, within the bound.
A program may use at most 256 MiB of HBM per device.

v0:
```python
import jax
import jax.numpy as jnp
from jax import lax
from jax.sharding import PartitionSpec as P

eps = 1e-05


def norm_rows(values, gain_vec, shift_vec):
    average = jnp.mean(values, axis=-1, keepdims=True)
    centred = values - average
    variance = jnp.mean(centred * centred, axis=-1, keepdims=True)
    return centred * lax.rsqrt(variance + eps) * gain_vec + shift_vec


def activation(values):
    return jax.nn.gelu(values, approximate=True)


def split_heads(values, head_count):
    row_count = values.shape[0]
    return values.reshape(row_count, head_count, values.shape[1] // head_count).transpose(1, 0, 2)


def join_heads(values):
    return values.transpose(1, 0, 2).reshape(values.shape[1], values.shape[0] * values.shape[2])


def score_rows(queries, key_rows, slope_h, positions, key_positions):
    scaling = queries.shape[1] ** (-0.5)
    scores = (
        jnp.einsum("qd,kd->qk", queries, key_rows, preferred_element_type=jnp.float32) * scaling
    )
    offset = (positions[:, None] - key_positions[None, :]).astype(jnp.float32)
    scores = scores - slope_h * offset
    return jnp.where(positions[:, None] >= key_positions[None, :], scores, -1000000000.0)


def attention_forward(queries, key_rows, value_rows, slopes, positions, key_positions):
    head_count = slopes.shape[0]

    def head_forward(operands):
        query_h, key_h, value_h, slope_h = operands
        scores = score_rows(query_h, key_h, slope_h, positions, key_positions)
        row_max = jnp.max(scores, axis=-1, keepdims=True)
        exponent = jnp.exp(scores - row_max)
        row_sum = jnp.sum(exponent, axis=-1, keepdims=True)
        probability = (exponent / row_sum).astype(jnp.bfloat16)
        context_h = jnp.dot(probability, value_h, preferred_element_type=jnp.float32)
        return (context_h, (row_max + jnp.log(row_sum))[:, 0])

    context_heads, log_totals = lax.map(
        head_forward,
        (
            split_heads(queries, head_count),
            split_heads(key_rows, head_count),
            split_heads(value_rows, head_count),
            slopes,
        ),
    )
    return (join_heads(context_heads).astype(jnp.bfloat16), log_totals)


def attention_backward(
    queries, key_rows, value_rows, grad_context, log_totals, slopes, positions, key_positions
):
    head_count = slopes.shape[0]

    def head_backward(operands):
        query_h, key_h, value_h, grad_ctx_h, log_h, slope_h = operands
        scaling = query_h.shape[1] ** (-0.5)
        scores = score_rows(query_h, key_h, slope_h, positions, key_positions)
        probability = jnp.exp(scores - log_h[:, None])
        grad_probs = jnp.einsum(
            "qd,kd->qk", grad_ctx_h, value_h, preferred_element_type=jnp.float32
        )
        inner_sum = jnp.sum(probability * grad_probs, axis=-1, keepdims=True)
        grad_scores = (probability * (grad_probs - inner_sum)).astype(jnp.bfloat16)
        grad_query = jnp.dot(grad_scores, key_h, preferred_element_type=jnp.float32) * scaling
        grad_key = (
            jnp.einsum("qk,qd->kd", grad_scores, query_h, preferred_element_type=jnp.float32)
            * scaling
        )
        grad_value = jnp.einsum(
            "qk,qd->kd",
            probability.astype(jnp.bfloat16),
            grad_ctx_h,
            preferred_element_type=jnp.float32,
        )
        return (grad_query, grad_key, grad_value)

    grad_query_h, grad_key_h, grad_value_h = lax.map(
        head_backward,
        (
            split_heads(queries, head_count),
            split_heads(key_rows, head_count),
            split_heads(value_rows, head_count),
            split_heads(grad_context, head_count),
            log_totals,
            slopes,
        ),
    )
    return (join_heads(grad_query_h), join_heads(grad_key_h), join_heads(grad_value_h))


def fetch_weights(own_part):
    return (
        lax.all_gather(own_part[0], "shard", axis=0, tiled=True),
        lax.all_gather(own_part[1], "shard", axis=0, tiled=True),
        lax.all_gather(own_part[2], "shard", axis=0, tiled=True),
        lax.all_gather(own_part[3], "shard", axis=0, tiled=True),
        lax.all_gather(own_part[4], "shard", axis=0, tiled=True),
        lax.all_gather(own_part[5], "shard", axis=0, tiled=True),
        lax.all_gather(own_part[6], "shard", axis=0, tiled=True),
        lax.all_gather(own_part[7], "shard", axis=0, tiled=True),
        lax.all_gather(own_part[8], "shard", axis=0, tiled=True),
        lax.all_gather(own_part[9], "shard", axis=0, tiled=True),
        lax.all_gather(own_part[10], "shard", axis=0, tiled=True),
        lax.all_gather(own_part[11], "shard", axis=0, tiled=True),
        lax.all_gather(own_part[12], "shard", axis=0, tiled=True),
    )


def fetch_again(own_part):
    return (
        lax.all_gather(own_part[0], "shard", axis=0, tiled=True),
        lax.all_gather(own_part[1], "shard", axis=0, tiled=True),
        lax.all_gather(own_part[2], "shard", axis=0, tiled=True),
        lax.all_gather(own_part[3], "shard", axis=0, tiled=True),
        lax.all_gather(own_part[4], "shard", axis=0, tiled=True),
        lax.all_gather(own_part[5], "shard", axis=0, tiled=True),
        lax.all_gather(own_part[6], "shard", axis=0, tiled=True),
        lax.all_gather(own_part[7], "shard", axis=0, tiled=True),
        lax.all_gather(own_part[8], "shard", axis=0, tiled=True),
        lax.all_gather(own_part[9], "shard", axis=0, tiled=True),
        lax.all_gather(own_part[10], "shard", axis=0, tiled=True),
        lax.all_gather(own_part[11], "shard", axis=0, tiled=True),
        lax.all_gather(own_part[12], "shard", axis=0, tiled=True),
    )


def share_grads(gradients):
    return (
        lax.psum_scatter(
            gradients[0].astype(jnp.bfloat16), "shard", scatter_dimension=0, tiled=True
        ).astype(jnp.float32),
        lax.psum_scatter(
            gradients[1].astype(jnp.bfloat16), "shard", scatter_dimension=0, tiled=True
        ).astype(jnp.float32),
        lax.psum_scatter(
            gradients[2].astype(jnp.bfloat16), "shard", scatter_dimension=0, tiled=True
        ).astype(jnp.float32),
        lax.psum_scatter(
            gradients[3].astype(jnp.bfloat16), "shard", scatter_dimension=0, tiled=True
        ).astype(jnp.float32),
        lax.psum_scatter(
            gradients[4].astype(jnp.bfloat16), "shard", scatter_dimension=0, tiled=True
        ).astype(jnp.float32),
        lax.psum_scatter(
            gradients[5].astype(jnp.bfloat16), "shard", scatter_dimension=0, tiled=True
        ).astype(jnp.float32),
        lax.psum_scatter(
            gradients[6].astype(jnp.bfloat16), "shard", scatter_dimension=0, tiled=True
        ).astype(jnp.float32),
        lax.psum_scatter(
            gradients[7].astype(jnp.bfloat16), "shard", scatter_dimension=0, tiled=True
        ).astype(jnp.float32),
        lax.psum_scatter(
            gradients[8].astype(jnp.bfloat16), "shard", scatter_dimension=0, tiled=True
        ).astype(jnp.float32),
        lax.psum_scatter(
            gradients[9].astype(jnp.bfloat16), "shard", scatter_dimension=0, tiled=True
        ).astype(jnp.float32),
        lax.psum_scatter(
            gradients[10].astype(jnp.bfloat16), "shard", scatter_dimension=0, tiled=True
        ).astype(jnp.float32),
        lax.psum_scatter(
            gradients[11].astype(jnp.bfloat16), "shard", scatter_dimension=0, tiled=True
        ).astype(jnp.float32),
        lax.psum_scatter(
            gradients[12].astype(jnp.bfloat16), "shard", scatter_dimension=0, tiled=True
        ).astype(jnp.float32),
    )


def replica_layer(shares):
    return (
        lax.psum(shares[0].astype(jnp.bfloat16), "replica").astype(jnp.float32),
        lax.psum(shares[1].astype(jnp.bfloat16), "replica").astype(jnp.float32),
        lax.psum(shares[2].astype(jnp.bfloat16), "replica").astype(jnp.float32),
        lax.psum(shares[3].astype(jnp.bfloat16), "replica").astype(jnp.float32),
        lax.psum(shares[4].astype(jnp.bfloat16), "replica").astype(jnp.float32),
        lax.psum(shares[5].astype(jnp.bfloat16), "replica").astype(jnp.float32),
        lax.psum(shares[6].astype(jnp.bfloat16), "replica").astype(jnp.float32),
        lax.psum(shares[7].astype(jnp.bfloat16), "replica").astype(jnp.float32),
        lax.psum(shares[8].astype(jnp.bfloat16), "replica").astype(jnp.float32),
        lax.psum(shares[9].astype(jnp.bfloat16), "replica").astype(jnp.float32),
        lax.psum(shares[10].astype(jnp.bfloat16), "replica").astype(jnp.float32),
        lax.psum(shares[11].astype(jnp.bfloat16), "replica").astype(jnp.float32),
        lax.psum(shares[12].astype(jnp.bfloat16), "replica").astype(jnp.float32),
    )


def layer_forward(hidden, gathered, slopes, positions):
    (
        gain_a,
        shift_a,
        w_qkv,
        bias_q,
        bias_v,
        w_dense,
        bias_dense,
        gain_b,
        shift_b,
        w_up,
        bias_up,
        w_down,
        bias_down,
    ) = gathered
    features = hidden.shape[1]
    normed_a, pull_a = jax.vjp(
        norm_rows, hidden, gain_a.astype(jnp.float32), shift_a.astype(jnp.float32)
    )
    input_a = normed_a.astype(jnp.bfloat16)
    bias_all = jnp.concatenate(
        [
            bias_q.astype(jnp.float32),
            jnp.zeros((features,), jnp.float32),
            bias_v.astype(jnp.float32),
        ]
    )
    projected = (jnp.dot(input_a, w_qkv, preferred_element_type=jnp.float32) + bias_all).astype(
        jnp.bfloat16
    )
    queries = projected[:, :features]
    key_rows, value_rows = (
        lax.all_gather(projected[:, features : 2 * features], "shard", axis=0, tiled=True),
        lax.all_gather(projected[:, 2 * features :], "shard", axis=0, tiled=True),
    )
    key_positions = jnp.arange(key_rows.shape[0])
    context, log_totals = attention_forward(
        queries, key_rows, value_rows, slopes, positions, key_positions
    )
    after_attn = hidden + (
        jnp.dot(context, w_dense, preferred_element_type=jnp.float32)
        + bias_dense.astype(jnp.float32)
    )
    normed_b, pull_b = jax.vjp(
        norm_rows, after_attn, gain_b.astype(jnp.float32), shift_b.astype(jnp.float32)
    )
    input_b = normed_b.astype(jnp.bfloat16)
    pre_act = jnp.dot(input_b, w_up, preferred_element_type=jnp.float32) + bias_up.astype(
        jnp.float32
    )
    activated, pull_act = jax.vjp(activation, pre_act)
    active_b = activated.astype(jnp.bfloat16)
    result = after_attn + (
        jnp.dot(active_b, w_down, preferred_element_type=jnp.float32)
        + bias_down.astype(jnp.float32)
    )
    stored = (
        pull_a,
        input_a,
        queries,
        key_rows,
        value_rows,
        log_totals,
        context,
        pull_b,
        input_b,
        pull_act,
        active_b,
    )
    return (result, stored)


def layer_backward(grad_stream, gathered, stored, slopes, positions):
    (
        gain_a,
        shift_a,
        w_qkv,
        bias_q,
        bias_v,
        w_dense,
        bias_dense,
        gain_b,
        shift_b,
        w_up,
        bias_up,
        w_down,
        bias_down,
    ) = gathered
    (
        pull_a,
        input_a,
        queries,
        key_rows,
        value_rows,
        log_totals,
        context,
        pull_b,
        input_b,
        pull_act,
        active_b,
    ) = stored
    features = queries.shape[1]
    grad_mlp = grad_stream.astype(jnp.bfloat16)
    grad_bias_down = jnp.sum(grad_mlp.astype(jnp.float32), axis=0)
    grad_w_down = jnp.dot(active_b.T, grad_mlp, preferred_element_type=jnp.float32)
    grad_active = jnp.dot(grad_mlp, w_down.T, preferred_element_type=jnp.float32)
    grad_pre = pull_act(grad_active)[0].astype(jnp.bfloat16)
    grad_bias_up = jnp.sum(grad_pre.astype(jnp.float32), axis=0)
    grad_w_up = jnp.dot(input_b.T, grad_pre, preferred_element_type=jnp.float32)
    grad_input_b = jnp.dot(grad_pre, w_up.T, preferred_element_type=jnp.float32)
    back_b, grad_gain_b, grad_shift_b = pull_b(grad_input_b)
    grad_after = grad_stream + back_b
    grad_attn = grad_after.astype(jnp.bfloat16)
    grad_bias_dense = jnp.sum(grad_attn.astype(jnp.float32), axis=0)
    grad_w_dense = jnp.dot(context.T, grad_attn, preferred_element_type=jnp.float32)
    grad_context = jnp.dot(grad_attn, w_dense.T, preferred_element_type=jnp.float32).astype(
        jnp.bfloat16
    )
    key_positions = jnp.arange(key_rows.shape[0])
    grad_query, grad_key, grad_value = attention_backward(
        queries, key_rows, value_rows, grad_context, log_totals, slopes, positions, key_positions
    )
    key_terms = jnp.concatenate([grad_key, grad_value], axis=1)
    key_share = lax.psum_scatter(
        key_terms.astype(jnp.bfloat16), "shard", scatter_dimension=0, tiled=True
    ).astype(jnp.float32)
    grad_projected = jnp.concatenate([grad_query, key_share], axis=1).astype(jnp.bfloat16)
    grad_proj_wide = grad_projected.astype(jnp.float32)
    grad_bias_q = jnp.sum(grad_proj_wide[:, :features], axis=0)
    grad_bias_v = jnp.sum(grad_proj_wide[:, 2 * features :], axis=0)
    grad_w_qkv = jnp.dot(input_a.T, grad_projected, preferred_element_type=jnp.float32)
    grad_input_a = jnp.dot(grad_projected, w_qkv.T, preferred_element_type=jnp.float32)
    back_a, grad_gain_a, grad_shift_a = pull_a(grad_input_a)
    grad_before = grad_after + back_a
    gradients = (
        grad_gain_a,
        grad_shift_a,
        grad_w_qkv,
        grad_bias_q,
        grad_bias_v,
        grad_w_dense,
        grad_bias_dense,
        grad_gain_b,
        grad_shift_b,
        grad_w_up,
        grad_bias_up,
        grad_w_down,
        grad_bias_down,
    )
    return (grad_before, gradients)


def on_device(
    tokens,
    grad_out,
    slope_index,
    ln1_gain,
    ln1_bias,
    qkv_weight,
    q_bias,
    v_bias,
    dense_weight,
    dense_bias,
    ln2_gain,
    ln2_bias,
    up_weight,
    up_bias,
    down_weight,
    down_bias,
):
    parameters = (
        ln1_gain,
        ln1_bias,
        qkv_weight,
        q_bias,
        v_bias,
        dense_weight,
        dense_bias,
        ln2_gain,
        ln2_bias,
        up_weight,
        up_bias,
        down_weight,
        down_bias,
    )
    layer_count = qkv_weight.shape[0]
    row_count = tokens.shape[0]
    head_count = slope_index.shape[0]
    slopes = jnp.exp2(-8.0 * (slope_index.astype(jnp.float32) + 1.0) / head_count)
    hidden = tokens.astype(jnp.float32)
    grad_stream = grad_out.astype(jnp.float32)
    shares_all = [None] * layer_count
    positions = lax.axis_index("shard") * row_count + jnp.arange(row_count)
    stored_all = []
    gathered_all = []
    for layer_id in range(layer_count):
        gathered = fetch_weights(tuple((member[layer_id] for member in parameters)))
        hidden, stored = layer_forward(hidden, gathered, slopes, positions)
        stored_all.append(stored)
        gathered_all.append(gathered)
    for layer_id in reversed(range(layer_count)):
        gathered = fetch_again(tuple((member[layer_id] for member in parameters)))
        grad_stream, gradients = layer_backward(
            grad_stream, gathered, stored_all[layer_id], slopes, positions
        )
        shares = share_grads(gradients)
        shares = replica_layer(shares)
        shares_all[layer_id] = shares
    stacked = tuple(
        (
            jnp.stack([shares_one[member_id] for shares_one in shares_all])
            for member_id in range(len(parameters))
        )
    )
    return (hidden, grad_stream) + tuple(stacked)


def solution(mesh):
    placed = (
        P(("replica", "shard"), None),
        P(("replica", "shard"), None),
        P(),
        P(None, "shard"),
        P(None, "shard"),
        P(None, "shard", None),
        P(None, "shard"),
        P(None, "shard"),
        P(None, "shard", None),
        P(None, "shard"),
        P(None, "shard"),
        P(None, "shard"),
        P(None, "shard", None),
        P(None, "shard"),
        P(None, "shard", None),
        P(None, "shard"),
    )
    return jax.shard_map(
        on_device,
        mesh=mesh,
        in_specs=placed,
        out_specs=(
            P(("replica", "shard"), None),
            P(("replica", "shard"), None),
            P(None, "shard"),
            P(None, "shard"),
            P(None, "shard", None),
            P(None, "shard"),
            P(None, "shard"),
            P(None, "shard", None),
            P(None, "shard"),
            P(None, "shard"),
            P(None, "shard"),
            P(None, "shard", None),
            P(None, "shard"),
            P(None, "shard", None),
            P(None, "shard"),
        ),
        check_vma=False,
    )
```

profile of v0, /device:TPU:1, one launch (start us, length us, event | category | flops | bytes accessed | tf_op | source)
XLA Modules:
  0.0 2056.3 jit_solution(4090875159365202591)
XLA Ops:
  10.0 16.0 all-gather.16
  26.0 13.1 all-gather.17
  39.2 14.6 all-gather.3
  53.7 13.1 all-gather.4
  66.9 14.6 all-gather
  106.4 13.0 all-gather.6
  131.5 14.6 all-gather.8
  146.2 19.6 all-gather.10
  178.2 14.5 all-gather.13
  218.2 66.1 %while.60 = (s32[]{:T(128)}, bf16[16,128,64]{1,2,0:T(8,128)(2,1)S(1)}, f32[16,128]{1,0:T(8,128)S(1)}, bf16[16,128,64]{2,1,0:T(8,128)(2,1)}, bf16[16,1024,64]{2,1...) while((s32[]{:T(128)}, ...), condition=%wide.region_5.6_spmd.clone.clone, body=%wide.region_2.5_spmd.clone.clone.sunk | while | flops 35258368 | bytes 2171513 | solution.py:52
  286.8 48.5 %all-gather.51.cloned.1.call-done = bf16[1,1024,4096]{2,1,0:T(8,128)(2,1)} async-done(((bf16[1,128,4096]{2,1,0:T(8,128)(2,1)}), bf16[1,1024,4096]{2,1,0:T(8,128)(2,1)}) %all-gather.51.cloned.1.call-update) | async-done | bytes 8388624 | tf_op jit(solution)/shard_map/all_gather | solution.py:117
  341.3 86.2 %all-gather.53.cloned.1.call-done = bf16[1,4096,1024]{2,1,0:T(8,128)(2,1)} async-done(((bf16[1,512,1024]{2,1,0:T(8,128)(2,1)}), bf16[1,4096,1024]{2,1,0:T(8,128)(2,1)}) %all-gather.53.cloned.1.call-update) | async-done | bytes 8388624 | tf_op jit(solution)/shard_map/all_gather | solution.py:119
  433.4 66.8 %all-gather.55.cloned.1.call-done = bf16[1,1024,3072]{2,1,0:T(8,128)(2,1)} async-done(((bf16[1,128,3072]{2,1,0:T(8,128)(2,1)}), bf16[1,1024,3072]{2,1,0:T(8,128)(2,1)}) %all-gather.55.cloned.1.call-update) | async-done | bytes 6291472 | tf_op jit(solution)/shard_map/all_gather | solution.py:110
  520.1 14.4 all-gather.20
  547.2 20.4 all-gather.23
  591.7 65.8 %while.61 = (s32[]{:T(128)}, bf16[16,128,64]{1,2,0:T(8,128)(2,1)S(1)}, f32[16,128]{1,0:T(8,128)S(1)}, bf16[16,128,64]{2,1,0:T(8,128)(2,1)S(1)}, bf16[16,1024,64]...) while((s32[]{:T(128)}, ...), condition=%wide.region_13.14_spmd.clone.clone, body=%wide.region_10.13_spmd.clone.clone.sunk | while | flops 35258368 | bytes 2171513 | solution.py:52
  660.1 63.6 %all-gather.59.cloned.1.call-done = bf16[1,1024,4096]{2,1,0:T(8,128)(2,1)} async-done(((bf16[1,128,4096]{2,1,0:T(8,128)(2,1)}), bf16[1,1024,4096]{2,1,0:T(8,128)(2,1)}) %all-gather.59.cloned.1.call-update) | async-done | bytes 8388624 | tf_op jit(solution)/shard_map/all_gather | solution.py:117
  729.8 86.7 %all-gather.61.cloned.1.call-done = bf16[1,4096,1024]{2,1,0:T(8,128)(2,1)} async-done(((bf16[1,512,1024]{2,1,0:T(8,128)(2,1)}), bf16[1,4096,1024]{2,1,0:T(8,128)(2,1)}) %all-gather.61.cloned.1.call-update) | async-done | bytes 8388624 | tf_op jit(solution)/shard_map/all_gather | solution.py:119
  833.9 134.4 %while.62 = (s32[]{:T(128)}, bf16[16,128,64]{1,2,0:T(8,128)(2,1)S(1)}, bf16[16,1024,64]{1,2,0:T(8,128)(2,1)}, bf16[16,1024,64]{1,2,0:T(8,128)(2,1)}, bf16[16,128...) while((s32[]{:T(128)}, ...), condition=%wide.region_20.21_spmd.clone.clone, body=%wide.region_18.20_spmd.clone.clone.sunk | while | flops 85794816 | bytes 5383305 | solution.py:92
  979.9 51.8 %reduce-scatter.31.cloned.1.call-done = bf16[128,2048]{1,0:T(8,128)(2,1)} async-done(((bf16[1024,2048]{1,0:T(8,128)(2,1)}), bf16[128,2048]{1,0:T(8,128)(2,1)}) %reduce-scatter.31.cloned.1.call-update) | async-done | bytes 524304
  1058.8 134.4 %while.63 = (s32[]{:T(128)}, bf16[16,128,64]{1,2,0:T(8,128)(2,1)S(1)}, bf16[16,1024,64]{1,2,0:T(8,128)(2,1)}, bf16[16,1024,64]{1,2,0:T(8,128)(2,1)}, bf16[16,128...) while((s32[]{:T(128)}, ...), condition=%wide.region_28.29_spmd.clone.clone, body=%wide.region_26.28_spmd.clone.clone.sunk | while | flops 85794816 | bytes 5383305 | solution.py:92
  1262.5 33.2 %reduce-scatter.21.cloned.1.call-done = bf16[128,1024]{1,0:T(8,128)(2,1)} async-done(((bf16[1024,1024]{1,0:T(8,128)(2,1)}), bf16[128,1024]{1,0:T(8,128)(2,1)}) %reduce-scatter.21.cloned.1.call-update) | async-done | bytes 262160 | tf_op jit(solution)/shard_map/reduce_scatter | solution.py:159
  1295.7 43.6 %reduce-scatter.19.cloned.1.call-done = bf16[128,1024]{1,0:T(8,128)(2,1)} async-done(((bf16[1024,1024]{1,0:T(8,128)(2,1)}), bf16[128,1024]{1,0:T(8,128)(2,1)}) %reduce-scatter.19.cloned.1.call-update) | async-done | bytes 262160 | tf_op jit(solution)/shard_map/reduce_scatter | solution.py:159
  1339.4 98.8 %reduce-scatter.25.cloned.1.call-done = bf16[128,4096]{1,0:T(8,128)(2,1)} async-done(((bf16[1024,4096]{1,0:T(8,128)(2,1)}), bf16[128,4096]{1,0:T(8,128)(2,1)}) %reduce-scatter.25.cloned.1.call-update) | async-done | bytes 1048592 | tf_op jit(solution)/shard_map/reduce_scatter | solution.py:171
  1438.2 93.8 %reduce-scatter.29.cloned.1.call-done = bf16[512,1024]{1,0:T(8,128)(2,1)} async-done(((bf16[4096,1024]{1,0:T(8,128)(2,1)}), bf16[512,1024]{1,0:T(8,128)(2,1)}) %reduce-scatter.29.cloned.1.call-update) | async-done | bytes 1048592 | tf_op jit(solution)/shard_map/reduce_scatter | solution.py:177
  1532.0 74.1 %reduce-scatter.17.cloned.1.call-done = bf16[128,3072]{1,0:T(8,128)(2,1)} async-done(((bf16[1024,3072]{1,0:T(8,128)(2,1)}), bf16[128,3072]{1,0:T(8,128)(2,1)}) %reduce-scatter.17.cloned.1.call-update) | async-done | bytes 786448 | tf_op jit(solution)/shard_map/reduce_scatter | solution.py:150
  1606.1 93.8 %reduce-scatter.23.cloned.1.call-done = bf16[128,4096]{1,0:T(8,128)(2,1)} async-done(((bf16[1024,4096]{1,0:T(8,128)(2,1)}), bf16[128,4096]{1,0:T(8,128)(2,1)}) %reduce-scatter.23.cloned.1.call-update) | async-done | bytes 1048592 | tf_op jit(solution)/shard_map/reduce_scatter | solution.py:171
  1699.9 93.9 %reduce-scatter.27.cloned.1.call-done = bf16[512,1024]{1,0:T(8,128)(2,1)} async-done(((bf16[4096,1024]{1,0:T(8,128)(2,1)}), bf16[512,1024]{1,0:T(8,128)(2,1)}) %reduce-scatter.27.cloned.1.call-update) | async-done | bytes 1048592 | tf_op jit(solution)/shard_map/reduce_scatter | solution.py:177
  1793.8 74.1 %reduce-scatter.15.cloned.1.call-done = bf16[128,3072]{1,0:T(8,128)(2,1)} async-done(((bf16[1024,3072]{1,0:T(8,128)(2,1)}), bf16[128,3072]{1,0:T(8,128)(2,1)}) %reduce-scatter.15.cloned.1.call-update) | async-done | bytes 786448 | tf_op jit(solution)/shard_map/reduce_scatter | solution.py:150
  1894.2 28.6 %all-reduce.20 = (bf16[1024]{0:T(1024)(128)(2,1)S(1)}, bf16[1024]{0:T(1024)(128)(2,1)S(1)}, bf16[1024]{0:T(1024)(128)(2,1)S(1)}, bf16[1024]{0:T(1024)(128)(2,1)S...) all-reduce(bf16[1024]{0:T(1024)(128)(2,1)S(1)} %get-tuple-element.5, ...), channel_id=31, replica_groups=mesh['replica'=16,'shard'=8] {'shard'}, use_global_device_ids=true, to_apply=%region_36.37.clone | all-reduce | flops 24576 | bytes 98304
  1923.6 67.8 %all-reduce.18 = (bf16[1,128]{1,0:T(2,128)(2,1)S(1)}, bf16[1,128]{1,0:T(2,128)(2,1)S(1)}, bf16[1,128]{1,0:T(2,128)(2,1)S(1)}, bf16[1,128]{1,0:T(2,128)(2,1)S(1)}...) all-reduce(bf16[1,128]{1,0:T(2,128)(2,1)S(1)} %get-tuple-element.74, ...), channel_id=1, replica_groups=mesh['replica'=16,'shard'=8] {'replica'}, use_global_device_ids=true, to_apply=%region_37.38 | all-reduce | flops 3072 | bytes 12288 | tf_op jit(solution)/shard_map/psum | solution.py:188
  1998.8 40.6 %all-reduce.23.cloned.1.call-done = (bf16[1,128,3072]{2,1,0:T(8,128)(2,1)}, bf16[1,128,3072]{2,1,0:T(8,128)(2,1)}, bf16[1,128,1024]{2,1,0:T(8,128)(2,1)}, bf16[1...) async-done(((bf16[1,128,3072]{2,1,0:T(8,128)(2,1)}, ...) | async-done | bytes 6291472 | tf_op jit(solution)/shard_map/psum | solution.py:190
  (834 shorter events, 723.5 us)
Async XLA Ops:
  7.2 59.6 %copy-start.41 = (bf16[2,128]{1,0:T(2,128)(2,1)S(1)}, bf16[2,128]{1,0:T(2,128)(2,1)}, u32[]{:S(2)}) copy-start(bf16[2,128]{1,0:T(2,128)(2,1)} %param.27) | copy-start | bytes 1540
  7.2 74.2 %copy-start.42 = (bf16[2,128]{1,0:T(2,128)(2,1)S(1)}, bf16[2,128]{1,0:T(2,128)(2,1)}, u32[]{:S(2)}) copy-start(bf16[2,128]{1,0:T(2,128)(2,1)} %param.28) | copy-start | bytes 1540
  7.2 85.8 %copy-start.1 = (bf16[128,1024]{1,0:T(8,128)(2,1)S(1)}, bf16[128,1024]{1,0:T(8,128)(2,1)}, u32[]{:S(2)}) copy-start(bf16[128,1024]{1,0:T(8,128)(2,1)} %param.24) | copy-start | bytes 786436
  7.2 86.1 %all-gather.47.cloned.1.call-start = ((), (), s32[]{:S(2)}) async-start(), calls=%async_computation.22 | async-start | bytes 7077888 | tf_op jit(solution)/shard_map/all_gather | solution.py:110
  10.0 196.2 %all-gather.39.cloned.1.call-start = ((), (), s32[]{:S(2)}) async-start(), calls=%async_computation.10 | async-start | bytes 2359296 | tf_op jit(solution)/shard_map/all_gather | solution.py:237
  98.2 114.0 %all-gather.41.cloned.1.call-start = ((), (), s32[]{:S(2)}) async-start(), calls=%async_computation.11 | async-start | bytes 2359296 | tf_op jit(solution)/shard_map/all_gather | solution.py:238
  98.9 185.4 %all-gather.49.cloned.1.call-start = ((), (), s32[]{:S(2)}) async-start(), calls=%async_computation.23 | async-start | bytes 2359296 | tf_op jit(solution)/shard_map/all_gather | solution.py:113
  100.8 234.4 %all-gather.51.cloned.1.call-start = ((), (), s32[]{:S(2)}) async-start(), calls=%async_computation.24 | async-start | bytes 9437184 | tf_op jit(solution)/shard_map/all_gather | solution.py:117
  102.4 63.4 %copy-start.46 = (bf16[2,128]{1,0:T(2,128)(2,1)S(1)}, bf16[2,128]{1,0:T(2,128)(2,1)}, u32[]{:S(2)}) copy-start(bf16[2,128]{1,0:T(2,128)(2,1)} %param.39) | copy-start | bytes 1540
  102.4 325.1 %all-gather.53.cloned.1.call-start = ((), (), s32[]{:S(2)}) async-start(), calls=%async_computation.25 | async-start | bytes 9437184 | tf_op jit(solution)/shard_map/all_gather | solution.py:119
  105.5 394.6 %all-gather.55.cloned.1.call-start = ((), (), s32[]{:S(2)}) async-start(), calls=%async_computation.26 | async-start | bytes 7077888 | tf_op jit(solution)/shard_map/all_gather | solution.py:110
  106.3 461.8 %all-gather.43.cloned.1.call-start = ((), (), s32[]{:S(2)}) async-start(), calls=%async_computation.12 | async-start | bytes 2359296 | tf_op jit(solution)/shard_map/all_gather | solution.py:237
  504.9 78.0 %all-gather.45.cloned.1.call-start = ((), (), s32[]{:S(2)}) async-start(), calls=%async_computation.13 | async-start | bytes 2359296 | tf_op jit(solution)/shard_map/all_gather | solution.py:238
  505.7 151.9 %all-gather.57.cloned.1.call-start = ((), (), s32[]{:S(2)}) async-start(), calls=%async_computation.27 | async-start | bytes 2359296 | tf_op jit(solution)/shard_map/all_gather | solution.py:113
  506.2 217.5 %all-gather.59.cloned.1.call-start = ((), (), s32[]{:S(2)}) async-start(), calls=%async_computation.28 | async-start | bytes 9437184 | tf_op jit(solution)/shard_map/all_gather | solution.py:117
  507.0 309.5 %all-gather.61.cloned.1.call-start = ((), (), s32[]{:S(2)}) async-start(), calls=%async_computation.29 | async-start | bytes 9437184 | tf_op jit(solution)/shard_map/all_gather | solution.py:119
  507.6 524.2 %reduce-scatter.31.cloned.1.call-start = ((), (), s32[]{:S(2)}) async-start(), calls=%async_computation.30 | async-start | bytes 4718592
  657.5 72.3 %copy-start.23 = (bf16[16,128,64]{1,2,0:T(8,128)(2,1)}, bf16[16,128,64]{1,2,0:T(8,128)(2,1)S(1)}, u32[]{:S(2)}) copy-start(bf16[16,128,64]{1,2,0:T(8,128)(2,1)S(1)} %get-tuple-element.252) | copy-start | bytes 786436
  657.5 72.3 %copy-start.33 = (bf16[16,128,64]{2,1,0:T(8,128)(2,1)}, bf16[16,128,64]{2,1,0:T(8,128)(2,1)S(1)}, u32[]{:S(2)}) copy-start(bf16[16,128,64]{2,1,0:T(8,128)(2,1)S(1)} %get-tuple-element.1242) | copy-start | bytes 786436
  723.7 92.8 %copy-start.16 = (bf16[128,1024]{1,0:T(8,128)(2,1)S(1)}, bf16[128,1024]{1,0:T(8,128)(2,1)}, u32[]{:S(2)}) copy-start(bf16[128,1024]{1,0:T(8,128)(2,1)} %param.25) | copy-start | bytes 786436
  968.4 64.7 %copy-start.20 = (bf16[16,128,64]{1,2,0:T(8,128)(2,1)}, bf16[16,128,64]{1,2,0:T(8,128)(2,1)S(1)}, u32[]{:S(2)}) copy-start(bf16[16,128,64]{1,2,0:T(8,128)(2,1)S(1)} %get-tuple-element.254) | copy-start | bytes 786436
  979.7 276.8 %reduce-scatter.33.cloned.1.call-start = ((), (), s32[]{:S(2)}) async-start(), calls=%async_computation.31 | async-start | bytes 4718592
  1033.0 192.0 %copy-start.8 = (bf16[128,2048]{0,1:T(8,128)(2,1)}, bf16[128,2048]{0,1:T(8,128)(2,1)S(1)}, u32[]{:S(2)}) copy-start(bf16[128,2048]{0,1:T(8,128)(2,1)S(1)} %copy.84) | copy-start | bytes 1572868
  1204.5 91.3 %reduce-scatter.21.cloned.1.call-start = ((), (), s32[]{:S(2)}) async-start(), calls=%async_computation.17 | async-start | bytes 2359296 | tf_op jit(solution)/shard_map/reduce_scatter | solution.py:159
  1207.5 131.9 %reduce-scatter.19.cloned.1.call-start = ((), (), s32[]{:S(2)}) async-start(), calls=%async_computation.16 | async-start | bytes 2359296 | tf_op jit(solution)/shard_map/reduce_scatter | solution.py:159
  1210.5 227.7 %reduce-scatter.25.cloned.1.call-start = ((), (), s32[]{:S(2)}) async-start(), calls=%async_computation.19 | async-start | bytes 9437184 | tf_op jit(solution)/shard_map/reduce_scatter | solution.py:171
  1217.7 314.3 %reduce-scatter.29.cloned.1.call-start = ((), (), s32[]{:S(2)}) async-start(), calls=%async_computation.21 | async-start | bytes 9437184 | tf_op jit(solution)/shard_map/reduce_scatter | solution.py:177
  1225.0 381.1 %reduce-scatter.17.cloned.1.call-start = ((), (), s32[]{:S(2)}) async-start(), calls=%async_computation.15 | async-start | bytes 7077888 | tf_op jit(solution)/shard_map/reduce_scatter | solution.py:150
  1230.6 469.3 %reduce-scatter.23.cloned.1.call-start = ((), (), s32[]{:S(2)}) async-start(), calls=%async_computation.18 | async-start | bytes 9437184 | tf_op jit(solution)/shard_map/reduce_scatter | solution.py:171
  1237.6 556.2 %reduce-scatter.27.cloned.1.call-start = ((), (), s32[]{:S(2)}) async-start(), calls=%async_computation.20 | async-start | bytes 9437184 | tf_op jit(solution)/shard_map/reduce_scatter | solution.py:177
  1244.9 623.0 %reduce-scatter.15.cloned.1.call-start = ((), (), s32[]{:S(2)}) async-start(), calls=%async_computation.14 | async-start | bytes 7077888 | tf_op jit(solution)/shard_map/reduce_scatter | solution.py:150
  1262.5 776.9 %all-reduce.23.cloned.1.call-start = ((), (), s32[]{:S(2)}) async-start(), calls=%async_computation.32 | async-start | bytes 12582912 | tf_op jit(solution)/shard_map/psum | solution.py:190
  (46 other events, 337.6 us)
Sparse Core Ops, SparseCore 0:
  10.3 75.6 all-gather.46
  98.3 53.1 all-gather.38
  153.7 40.7 all-gather.40
  196.0 40.9 all-gather.48
  239.1 96.1 all-gather.50
  336.8 90.6 all-gather.52
  429.1 71.0 all-gather.54
  505.0 35.5 all-gather.42
  542.9 39.9 all-gather.44
  584.4 41.2 all-gather.56
  627.3 96.3 all-gather.58
  725.8 90.6 all-gather.60
  979.8 51.8 reduce-scatter.30
  1204.6 51.8 reduce-scatter.32
  1259.3 36.3 reduce-scatter.20
  1298.0 41.3 reduce-scatter.18
  1341.6 96.5 reduce-scatter.24
  1440.5 91.4 reduce-scatter.28
  1534.4 71.6 reduce-scatter.16
  1608.4 91.4 reduce-scatter.22
  1702.3 91.4 reduce-scatter.26
  1796.2 71.6 reduce-scatter.14
  1871.0 168.3 all-reduce.22
where the time goes:
time: 2080 us; the launch traced here: 2060 us
  waiting for transfers between devices  1070 us (51%)
  matrix products  454 us (22%)
  blocking collectives  350 us (17%)
  local copies, waits for them, and re-layouts  119 us (6%)
  other arithmetic  41.6 us (2%)
    reduce_scatter x2, waiting for transfers between devices, share_grads(): lax.psum_scatter(gradients[9].astype(jnp.bfloat16), 'shard', scatter_dime...  193 us
    reduce_scatter x2, waiting for transfers between devices, share_grads(): lax.psum_scatter(gradients[11].astype(jnp.bfloat16), 'shard', scatter_dim...  188 us
    all_gather x2, waiting for transfers between devices, fetch_weights(): lax.all_gather(own_part[11], 'shard', axis=0, tiled=True)  173 us
    reduce_scatter x2, waiting for transfers between devices, share_grads(): lax.psum_scatter(gradients[2].astype(jnp.bfloat16), 'shard', scatter_dime...  148 us
    dot_general x64, matrix products, score_rows(): jnp.einsum('qd,kd->qk', queries, key_rows, preferred_element_type=jnp.flo...  129 us
    all_gather x2, waiting for transfers between devices, fetch_weights(): lax.all_gather(own_part[9], 'shard', axis=0, tiled=True)  112 us
    reduce_scatter x2, waiting for transfers between devices, share_grads(): lax.psum_scatter(gradients[5].astype(jnp.bfloat16), 'shard', scatter_dime...  76.8 us
    psum x1, blocking collectives, replica_layer(): lax.psum(shares[0].astype(jnp.bfloat16), 'replica').astype(jnp.float32)  67.8 us
  transfers between devices with their start and end apart: 23, of which 17 were waited for; matrix products, arithmetic and copies ran while one was open for 12% of the time, Pallas kernels for 0%

commit v1 on v0

v1 whole, which is shorter than its diff:
```python
import functools

import jax
import jax.numpy as jnp
from jax import lax
from jax.experimental import pallas as pl
from jax.experimental.pallas import tpu as pltpu
from jax.sharding import Mesh
from jax.sharding import PartitionSpec as P

eps = 1e-05
MESH = pl.DeviceIdType.MESH
AXES = ("z", "xh", "c", "xl", "y")
BF = jnp.bfloat16
F32 = jnp.float32
BLK = 128
HALF = 64
WIDTH = 1024
RING = 4
CALL_VMEM = 56 * 1024 * 1024


def gelu(u):
    t = jnp.tanh(0.7978845608028654 * (u + 0.044715 * u * u * u))
    return 0.5 * u * (1.0 + t)


def gelu_slope(u):
    sq = u * u
    t = jnp.tanh(0.7978845608028654 * (u + 0.044715 * sq * u))
    return 0.5 * (1.0 + t) + 0.5 * u * (1.0 - t * t) * (
        0.7978845608028654 * (1.0 + 3.0 * 0.044715 * sq)
    )


def norm_parts(values):
    average = jnp.mean(values, axis=-1, keepdims=True)
    centred = values - average
    variance = jnp.mean(centred * centred, axis=-1, keepdims=True)
    r = lax.rsqrt(variance + eps)
    return centred * r, r


def comm_kernel(cfg, names, *refs):
    ref = dict(zip(names, refs))
    y, c, xl = lax.axis_index("y"), lax.axis_index("c"), lax.axis_index("xl")
    up, down, far = lax.rem(y + 1, RING), lax.rem(y + 3, RING), lax.rem(y + 2, RING)
    oc, ox = 1 - c, 1 - xl
    sib, nxt, prv, xnb = {"c": oc}, {"y": up}, {"y": down}, {"xl": ox}
    partners = [sib, nxt, prv] + ([xnb] if cfg["swap_in"] or cfg["swap_out"] else [])

    barrier = pltpu.get_barrier_semaphore()
    for partner in partners:
        pl.semaphore_signal(barrier, inc=1, device_id=partner, device_id_type=MESH)
    pl.semaphore_wait(barrier, len(partners))

    sent = []

    def push(src, dst, target):
        i = len(sent)
        copy = pltpu.make_async_remote_copy(
            src_ref=src,
            dst_ref=dst,
            send_sem=ref["send"].at[i],
            recv_sem=ref["recv"].at[i],
            device_id=target,
            device_id_type=MESH,
        )
        copy.start()
        sent.append(copy)
        return copy

    local = []

    def store(src, dst):
        copy = pltpu.make_async_copy(src, dst, ref["local"].at[len(local)])
        copy.start()
        local.append(copy)

    def rows(group, q, offset=0, size=BLK):
        return pl.ds(pl.multiple_of((group * RING + q) * BLK + offset, HALF), size)

    def gather_start(block):
        own = rows(c, y)
        low, high = rows(c, y, 0, HALF), rows(c, y, HALF, HALF)
        gbuf = ref["gbuf"]
        gbuf[own, :] = block
        first = [
            push(gbuf.at[low], gbuf.at[low], nxt),
            push(gbuf.at[high], gbuf.at[high], prv),
            push(gbuf.at[own], gbuf.at[own], sib),
            push(gbuf.at[high], gbuf.at[high], nxt),
            push(gbuf.at[low], gbuf.at[low], prv),
        ]
        return first

    def gather_rest(first, consume):
        gbuf = ref["gbuf"]
        low_n, high_p, own_s, high_n, low_p = first
        consume(c, y)
        low_n.wait_recv()
        part = gbuf.at[rows(c, down, 0, HALF)]
        fwd_n = push(part, part, nxt)
        high_p.wait_recv()
        part = gbuf.at[rows(c, up, HALF, HALF)]
        fwd_p = push(part, part, prv)
        own_s.wait_recv()
        consume(oc, y)
        high_n.wait_recv()
        part = gbuf.at[rows(c, down)]
        sib_a = push(part, part, sib)
        low_p.wait_recv()
        part = gbuf.at[rows(c, up)]
        sib_b = push(part, part, sib)
        consume(c, down)
        consume(c, up)
        sib_a.wait_recv()
        consume(oc, down)
        sib_b.wait_recv()
        consume(oc, up)
        fwd_n.wait_recv()
        fwd_p.wait_recv()
        part = gbuf.at[rows(c, far)]
        sib_c = push(part, part, sib)
        consume(c, far)
        sib_c.wait_recv()
        consume(oc, far)

    first = None
    if cfg["mid"] == "fin":
        first = gather_start(ref["grad_out"][...])

    acc = None
    if cfg["rs"]:
        order = [far, up, down, y]
        lhs = ref["lhs"]
        chunks = []
        if cfg["swap_in"]:
            rowbuf = ref["rowbuf"]
            for q in order:
                chunks.append(push(lhs.at[rows(ox, q)], rowbuf.at[rows(xl, q)], xnb))
            mine = pl.ds(pl.multiple_of(xl * RING * BLK, BLK), RING * BLK)
            rowbuf[mine, :] = lhs[mine, :]
        else:
            rowbuf = lhs

        def partial(group, q):
            return jnp.dot(
                rowbuf[rows(group, q), :], ref["w_rs"][...], preferred_element_type=F32
            )

        own, sib_out, sib_in = ref["own"], ref["sib_out"], ref["sib_in"]
        stage = ref["stage"]
        near_n, near_p, far_n, far_p = ref["near_n"], ref["near_p"], ref["far_n"], ref["far_p"]
        low, high = pl.ds(0, HALF), pl.ds(HALF, HALF)
        ring = {}
        passed = []

        def begin(slot):
            if chunks:
                chunks[slot].wait_recv()
            sib_out[slot] = partial(oc, order[slot]).astype(BF)
            passed.append(push(sib_out.at[slot], sib_in.at[slot], sib))
            own[slot] = partial(c, order[slot])

        def finish(slot):
            passed[slot].wait_recv()
            total = own[slot] + sib_in[slot].astype(F32)
            if slot == 0:
                stage[0] = total.astype(BF)
                ring["fn"] = push(stage.at[0, low], far_n, nxt)
                ring["fp"] = push(stage.at[0, high], far_p, prv)
            elif slot == 1:
                stage[1, high, :] = total[HALF:].astype(BF)
                ring["nh"] = push(stage.at[1, high], near_n.at[high], nxt)
                own[1, low, :] = total[:HALF]
            elif slot == 2:
                stage[2, low, :] = total[:HALF].astype(BF)
                ring["pl"] = push(stage.at[2, low], near_p.at[low], prv)
                own[2, high, :] = total[HALF:]
            else:
                own[3] = total

        begin(0)
        begin(1)
        finish(0)
        begin(2)
        finish(1)
        begin(3)
        finish(2)
        ring["fn"].wait_recv()
        stage[1, low, :] = (own[1, low, :] + far_n[...].astype(F32)).astype(BF)
        ring["nl"] = push(stage.at[1, low], near_n.at[low], nxt)
        ring["fp"].wait_recv()
        stage[2, high, :] = (own[2, high, :] + far_p[...].astype(F32)).astype(BF)
        ring["ph"] = push(stage.at[2, high], near_p.at[high], prv)
        finish(3)
        if cfg["swap_in"]:
            store(rowbuf, ref["rows_out"])
        for key in ("nh", "pl", "nl", "ph"):
            ring[key].wait_recv()
        acc = own[3] + near_n[...].astype(F32) + near_p[...].astype(F32)

    block = None
    if cfg["mid"] == "ln":
        xhat, _ = norm_parts(ref["resid"][...].astype(F32))
        block = (xhat * ref["gain"][...] + ref["shift"][...]).astype(BF)
    elif cfg["mid"] == "fwd":
        hidden = ref["resid"][...].astype(F32) + (acc + ref["bias_rs"][...])
        ref["hidden"][...] = hidden
        xhat, _ = norm_parts(hidden)
        block = (xhat * ref["gain"][...] + ref["shift"][...]).astype(BF)
    elif cfg["mid"] == "fin":
        ref["hidden"][...] = ref["resid"][...].astype(F32) + (acc + ref["bias_rs"][...])
    elif cfg["mid"] == "bwd":
        xhat, r = norm_parts(ref["resid"][...].astype(F32))
        ref["g_gain"][...] = jnp.sum(acc * xhat, axis=0, keepdims=True)
        ref["g_shift"][...] = jnp.sum(acc, axis=0, keepdims=True)
        scaled = acc * ref["gain"][...]
        grad = ref["stream"][...].astype(F32) + r * (
            scaled
            - jnp.mean(scaled, axis=-1, keepdims=True)
            - xhat * jnp.mean(scaled * xhat, axis=-1, keepdims=True)
        )
        ref["hidden"][...] = grad
        block = grad.astype(BF)

    if cfg["tail"] is not None:
        if first is None:
            first = gather_start(block)
        done = {}
        out_copies = []

        def consume(group, q):
            where = rows(group, q)
            value = jnp.dot(ref["gbuf"][where, :], ref["w_ag"][...], preferred_element_type=F32)
            if cfg["tail"] == "up":
                pre = value + ref["bias_ag"][...]
                ref["pre"][where, :] = pre
                ref["active"][where, :] = gelu(pre).astype(BF)
            elif cfg["tail"] == "dpre":
                ref["grad_pre"][where, :] = (value * gelu_slope(ref["pre_in"][where, :])).astype(BF)
            else:
                if cfg["tail"] == "qkv":
                    value = value + ref["bias_ag"][...]
                pbuf, xbuf = ref["pbuf"], ref["xbuf"]
                pbuf[where, :] = value.astype(BF)
                key = id(q)
                done[key] = done.get(key, 0) + 1
                if done[key] == 2:
                    out_copies.append(push(pbuf.at[rows(ox, q)], xbuf.at[rows(xl, q)], xnb))
                    xbuf[rows(xl, q), :] = pbuf[rows(xl, q), :]

        gather_rest(first, consume)
        store(ref["gbuf"], ref["gathered"])
        if cfg["swap_out"]:
            for copy in out_copies:
                copy.wait_recv()
            ref["att"][...] = ref["xbuf"][...]
    for copy in sent:
        copy.wait_send()
    for copy in local:
        copy.wait()


def comm_call(cid, *, mid, rs=False, swap_in=False, tail=None, **operands):
    swap_out = tail in ("qkv", "gctx")
    cfg = dict(rs=rs, swap_in=swap_in, swap_out=swap_out, mid=mid, tail=tail)
    whole = pl.BlockSpec(memory_space=pltpu.VMEM)
    in_names = list(operands)
    total_rows = 2 * RING * BLK
    outs = {}
    scratch = {}
    flops = 0
    if rs:
        k = operands["lhs"].shape[1]
        flops += 2 * total_rows * k * WIDTH
        if swap_in:
            outs["rows_out"] = ((total_rows, k), BF, pl.ANY)
            scratch["rowbuf"] = pltpu.VMEM((total_rows, k), BF)
        scratch["own"] = pltpu.VMEM((RING, BLK, WIDTH), F32)
        scratch["sib_out"] = pltpu.VMEM((RING, BLK, WIDTH), BF)
        scratch["sib_in"] = pltpu.VMEM((RING, BLK, WIDTH), BF)
        scratch["stage"] = pltpu.VMEM((3, BLK, WIDTH), BF)
        scratch["near_n"] = pltpu.VMEM((BLK, WIDTH), BF)
        scratch["near_p"] = pltpu.VMEM((BLK, WIDTH), BF)
        scratch["far_n"] = pltpu.VMEM((HALF, WIDTH), BF)
        scratch["far_p"] = pltpu.VMEM((HALF, WIDTH), BF)
    if mid != "ln":
        outs["hidden"] = ((BLK, WIDTH), F32, pltpu.VMEM)
    if mid == "bwd":
        outs["g_gain"] = ((1, WIDTH), F32, pltpu.VMEM)
        outs["g_shift"] = ((1, WIDTH), F32, pltpu.VMEM)
    if tail is not None:
        n = operands["w_ag"].shape[1]
        flops += 2 * total_rows * n * WIDTH
        outs["gathered"] = ((total_rows, WIDTH), BF, pl.ANY)
        scratch["gbuf"] = pltpu.VMEM((total_rows, WIDTH), BF)
        if tail == "up":
            outs["pre"] = ((total_rows, n), F32, pltpu.VMEM)
            outs["active"] = ((total_rows, n), BF, pltpu.VMEM)
        elif tail == "dpre":
            outs["grad_pre"] = ((total_rows, n), BF, pltpu.VMEM)
        else:
            outs["att"] = ((total_rows, n), BF, pltpu.VMEM)
            scratch["pbuf"] = pltpu.VMEM((total_rows, n), BF)
            scratch["xbuf"] = pltpu.VMEM((total_rows, n), BF)
    scratch["send"] = pltpu.SemaphoreType.DMA((32,))
    scratch["recv"] = pltpu.SemaphoreType.DMA((32,))
    scratch["local"] = pltpu.SemaphoreType.DMA((2,))
    results = pl.pallas_call(
        functools.partial(comm_kernel, cfg, in_names + list(outs) + list(scratch)),
        out_shape=[jax.ShapeDtypeStruct(shape, dtype) for shape, dtype, _ in outs.values()],
        in_specs=[whole] * len(in_names),
        out_specs=[pl.BlockSpec(memory_space=space) for _, _, space in outs.values()],
        scratch_shapes=list(scratch.values()),
        cost_estimate=pl.CostEstimate(flops=flops, bytes_accessed=20_000_000, transcendentals=0),
        compiler_params=pltpu.CompilerParams(
            collective_id=cid, has_side_effects=True, vmem_limit_bytes=CALL_VMEM
        ),
    )(*operands.values())
    return dict(zip(outs, results))


QB = 256


def head_only(values, head):
    lane = lax.broadcasted_iota(jnp.int32, values.shape, 1)
    keep = (lane // 64) == head
    return jnp.where(keep, values, jnp.zeros_like(values))


def probs_of(q_pad, keys, slope, start):
    count = keys.shape[0]
    scores = lax.dot_general(
        keys, q_pad, (((1,), (1,)), ((), ())), preferred_element_type=F32
    )
    key_pos = lax.broadcasted_iota(jnp.int32, (count, QB), 0)
    query_pos = lax.broadcasted_iota(jnp.int32, (count, QB), 1) + start
    scores = scores + slope * key_pos.astype(F32)
    scores = jnp.where(key_pos <= query_pos, scores, -1000000000.0)
    top = jnp.max(scores, axis=0, keepdims=True)
    exponent = jnp.exp(scores - top)
    total = jnp.sum(exponent, axis=0, keepdims=True)
    return exponent * (1.0 / total)


def attention_fwd_kernel(slopes, qkv, ctx):
    value_t = qkv[:, 2 * BLK : 3 * BLK].astype(F32).T.astype(BF)
    for start in range(0, qkv.shape[0], QB):
        count = start + QB
        queries = qkv[start : start + QB, 0:BLK] * jnp.asarray(0.125, BF)
        keys = qkv[0:count, BLK : 2 * BLK]
        parts = []
        for head in range(2):
            probs = probs_of(head_only(queries, head), keys, slopes[head], start).astype(BF)
            ctx_t = jnp.dot(value_t[:, 0:count], probs, preferred_element_type=F32)
            parts.append(ctx_t[head * 64 : head * 64 + 64])
        ctx[start : start + QB, :] = jnp.concatenate(parts, axis=0).T.astype(BF)


def attention_bwd_kernel(slopes, qkv, gctx, dqkv, dk, dv):
    key_t = qkv[:, BLK : 2 * BLK].astype(F32).T.astype(BF)
    dk[...] = jnp.zeros_like(dk)
    dv[...] = jnp.zeros_like(dv)
    for start in range(0, qkv.shape[0], QB):
        count = start + QB
        queries = qkv[start : start + QB, 0:BLK] * jnp.asarray(0.125, BF)
        keys = qkv[0:count, BLK : 2 * BLK]
        values = qkv[0:count, 2 * BLK : 3 * BLK]
        grads = gctx[start : start + QB, :]
        parts = []
        for head in range(2):
            q_pad = head_only(queries, head)
            g_pad = head_only(grads, head)
            probs = probs_of(q_pad, keys, slopes[head], start)
            grad_probs = lax.dot_general(
                values, g_pad, (((1,), (1,)), ((), ())), preferred_element_type=F32
            )
            inner = jnp.sum(probs * grad_probs, axis=0, keepdims=True)
            grad_scores = (probs * (grad_probs - inner)).astype(BF)
            dk[0:count, :] += jnp.dot(grad_scores, q_pad, preferred_element_type=F32)
            dv[0:count, :] += jnp.dot(probs.astype(BF), g_pad, preferred_element_type=F32)
            dq_t = jnp.dot(key_t[:, 0:count], grad_scores, preferred_element_type=F32)
            parts.append(dq_t[head * 64 : head * 64 + 64] * 0.125)
        dqkv[start : start + QB, 0:BLK] = jnp.concatenate(parts, axis=0).T.astype(BF)
    dqkv[:, BLK : 2 * BLK] = dk[...].astype(BF)
    dqkv[:, 2 * BLK : 3 * BLK] = dv[...].astype(BF)


def attention_call(kernel, slopes, qkv, *more, width, scratch=()):
    whole = pl.BlockSpec(memory_space=pltpu.VMEM)
    return pl.pallas_call(
        kernel,
        out_shape=jax.ShapeDtypeStruct((qkv.shape[0], width), BF),
        in_specs=[pl.BlockSpec(memory_space=pltpu.SMEM), whole] + [whole] * len(more),
        out_specs=whole,
        scratch_shapes=list(scratch),
        cost_estimate=pl.CostEstimate(
            flops=4_000_000_000, bytes_accessed=2_000_000, transcendentals=2_000_000
        ),
        compiler_params=pltpu.CompilerParams(vmem_limit_bytes=CALL_VMEM),
    )(slopes, qkv, *more)


def attention_forward(slopes, qkv):
    return attention_call(attention_fwd_kernel, slopes, qkv, width=BLK)


def attention_backward(slopes, qkv, gctx):
    scratch = [pltpu.VMEM((qkv.shape[0], BLK), F32)] * 2
    return attention_call(
        attention_bwd_kernel, slopes, qkv, gctx, width=3 * BLK, scratch=scratch
    )


def columns_to_rank(own_rows, parts):
    c = lax.axis_index("c")
    depth, cols = own_rows.shape
    per = cols // (parts * 2 * RING)
    split = own_rows.reshape(depth, parts, 2, RING, per)
    split = lax.dynamic_index_in_dim(split, c, 2, keepdims=False)
    split = split.transpose(2, 0, 1, 3).reshape(RING, depth, parts * per)
    mine = lax.all_to_all(split, "y", 0, 0, tiled=True)
    mine = mine.reshape(RING * depth, parts * per)
    other = lax.ppermute(mine, "xl", [(0, 1), (1, 0)])
    xl = lax.axis_index("xl")
    return jnp.where(
        xl == 0,
        jnp.concatenate([mine, other], axis=0),
        jnp.concatenate([other, mine], axis=0),
    )


def rows_to_rank(own_rows):
    other = lax.ppermute(own_rows, ("c", "xl"), [(0, 1), (3, 2)])
    return jnp.where(lax.axis_index("c") == lax.axis_index("xl"), own_rows, other)


def rank_to_shard(value):
    other = lax.ppermute(value, "c", [(0, 1), (1, 0)])
    return jnp.where(lax.axis_index("c") == lax.axis_index("xl"), value, other)


def rank_sum(value):
    return lax.psum(value.astype(BF), ("z", "xh", "xl"))


def columns_to_shard(value, parts):
    rows, cols = value.shape
    split = value.reshape(2 * RING, rows // (2 * RING), cols)
    got = lax.all_to_all(split, ("c", "y"), 0, 0, tiled=True)
    per = cols // parts
    got = got.reshape(2 * RING, rows // (2 * RING), parts, per).transpose(1, 2, 0, 3)
    return rank_to_shard(got.reshape(rows // (2 * RING), 2 * RING * cols)).astype(F32)


def rows_to_shard(value):
    return rank_to_shard(value).astype(F32)


def weight_grad(left, right):
    return lax.dot_general(left, right, (((0,), (0,)), ((), ())), preferred_element_type=F32)


def on_device(
    tokens,
    grad_out,
    slope_index,
    ln1_gain,
    ln1_bias,
    qkv_weight,
    q_bias,
    v_bias,
    dense_weight,
    dense_bias,
    ln2_gain,
    ln2_bias,
    up_weight,
    up_bias,
    down_weight,
    down_bias,
):
    layers = qkv_weight.shape[0]
    heads = slope_index.shape[0]
    rank = lax.axis_index("c") * RING + lax.axis_index("y")
    slopes_all = jnp.exp2(-8.0 * (slope_index.astype(F32) + 1.0) / heads)
    slopes = lax.dynamic_slice(slopes_all, (rank * 2,), (2,))

    vectors = jnp.stack([ln1_gain, ln1_bias, dense_bias, ln2_gain, ln2_bias, down_bias])
    vectors = lax.all_gather(vectors, ("xl", "y"), axis=2, tiled=True).astype(F32)
    w_qkv = [columns_to_rank(qkv_weight[i], 3) for i in range(layers)]
    w_up = [columns_to_rank(up_weight[i], 1) for i in range(layers)]
    w_dense = [rows_to_rank(dense_weight[i]) for i in range(layers)]
    w_down = [rows_to_rank(down_weight[i]) for i in range(layers)]
    b_up = rows_to_rank(up_bias).astype(F32)
    b_q = rows_to_rank(q_bias).astype(F32)
    b_v = rows_to_rank(v_bias).astype(F32)

    def vector(number, i):
        return vectors[number, i][None, :]

    def bias_qkv(i):
        return jnp.concatenate([b_q[i], jnp.zeros_like(b_q[i]), b_v[i]])[None, :]

    streams, mids, saved = [tokens], [], []
    step = comm_call(
        1, mid="ln", tail="qkv", resid=tokens, gain=vector(0, 0), shift=vector(1, 0),
        w_ag=w_qkv[0], bias_ag=bias_qkv(0),
    )
    output = None
    for i in range(layers):
        keep = {"input_a": step["gathered"], "qkv": step["att"]}
        context = attention_forward(slopes, step["att"])
        step = comm_call(
            2, mid="fwd", rs=True, swap_in=True, tail="up", lhs=context, w_rs=w_dense[i],
            resid=streams[i], bias_rs=vector(2, i), gain=vector(3, i), shift=vector(4, i),
            w_ag=w_up[i], bias_ag=b_up[i][None, :],
        ) if i else comm_call(
            3, mid="fwd", rs=True, swap_in=True, tail="up", lhs=context, w_rs=w_dense[i],
            resid=streams[i], bias_rs=vector(2, i), gain=vector(3, i), shift=vector(4, i),
            w_ag=w_up[i], bias_ag=b_up[i][None, :],
        )
        mids.append(step["hidden"])
        keep.update(
            context=step["rows_out"], input_b=step["gathered"], pre=step["pre"],
            active=step["active"],
        )
        saved.append(keep)
        if i + 1 < layers:
            step = comm_call(
                4, mid="fwd", rs=True, tail="qkv", lhs=step["active"], w_rs=w_down[i],
                resid=mids[i], bias_rs=vector(5, i), gain=vector(0, i + 1),
                shift=vector(1, i + 1), w_ag=w_qkv[i + 1], bias_ag=bias_qkv(i + 1),
            )
            streams.append(step["hidden"])
        else:
            step = comm_call(
                5, mid="fin", rs=True, tail="dpre", lhs=step["active"], w_rs=w_down[i],
                resid=mids[i], bias_rs=vector(5, i), grad_out=grad_out,
                w_ag=w_down[i].T, pre_in=keep["pre"],
            )
            output = step["hidden"]

    grad_stream = grad_out
    grads = [None] * layers
    small = [None] * layers
    for i in reversed(range(layers)):
        keep = saved[i]
        grad_mlp, grad_pre = step["gathered"], step["grad_pre"]
        cols = rank * BLK
        bias_down = jnp.sum(
            lax.dynamic_slice_in_dim(grad_mlp, cols, BLK, 1).astype(F32), axis=0
        )
        g_down = weight_grad(keep["active"], grad_mlp)
        g_up = weight_grad(keep["input_b"], grad_pre)
        bias_up = jnp.sum(grad_pre.astype(F32), axis=0)
        step = comm_call(
            6, mid="bwd", rs=True, tail="gctx", lhs=grad_pre, w_rs=w_up[i].T,
            resid=mids[i], gain=vector(3, i), stream=grad_stream, w_ag=w_dense[i].T,
        ) if i else comm_call(
            7, mid="bwd", rs=True, tail="gctx", lhs=grad_pre, w_rs=w_up[i].T,
            resid=mids[i], gain=vector(3, i), stream=grad_stream, w_ag=w_dense[i].T,
        )
        grad_after, grad_attn = step["hidden"], step["gathered"]
        gain_b, shift_b = step["g_gain"], step["g_shift"]
        bias_dense = jnp.sum(
            lax.dynamic_slice_in_dim(grad_attn, cols, BLK, 1).astype(F32), axis=0
        )
        g_dense = weight_grad(keep["context"], grad_attn)
        dqkv = attention_backward(slopes, keep["qkv"], step["att"])
        bias_qv = jnp.sum(dqkv.astype(F32), axis=0)
        if i:
            step = comm_call(
                8, mid="bwd", rs=True, swap_in=True, tail="dpre", lhs=dqkv, w_rs=w_qkv[i].T,
                resid=streams[i], gain=vector(0, i), stream=grad_after,
                w_ag=w_down[i - 1].T, pre_in=saved[i - 1]["pre"],
            )
        else:
            step = comm_call(
                9, mid="bwd", rs=True, swap_in=True, lhs=dqkv, w_rs=w_qkv[i].T,
                resid=streams[i], gain=vector(0, i), stream=grad_after,
            )
        grad_stream = step["hidden"]
        g_qkv = weight_grad(keep["input_a"], step["rows_out"])
        flat = jnp.concatenate([bias_qv[:BLK], bias_qv[2 * BLK :], bias_dense, bias_up, bias_down])
        small[i] = rows_to_shard(rank_sum(flat))
        grads[i] = dict(
            qkv=columns_to_shard(rank_sum(g_qkv), 3),
            up=columns_to_shard(rank_sum(g_up), 1),
            dense=rows_to_shard(rank_sum(g_dense)),
            down=rows_to_shard(rank_sum(g_down)),
            norms=jnp.concatenate([step["g_gain"], step["g_shift"], gain_b, shift_b]),
        )
    norms = lax.psum(jnp.stack([g["norms"] for g in grads], axis=1), AXES)
    shard = lax.axis_index("xl") * RING + lax.axis_index("y")
    norms = lax.dynamic_slice_in_dim(norms, shard * BLK, BLK, 2)
    flat = jnp.stack(small)

    def stacked(name):
        return jnp.stack([g[name] for g in grads])

    ff = up_bias.shape[1]
    return (
        output,
        grad_stream,
        norms[0],
        norms[1],
        stacked("qkv"),
        flat[:, 0:BLK],
        flat[:, BLK : 2 * BLK],
        stacked("dense"),
        flat[:, 2 * BLK : 3 * BLK],
        norms[2],
        norms[3],
        stacked("up"),
        flat[:, 3 * BLK : 3 * BLK + ff],
        stacked("down"),
        flat[:, 3 * BLK + ff :],
    )


def solution(mesh):
    replica, shard = mesh.devices.shape
    fine = Mesh(mesh.devices.reshape(replica // 4, 2, 2, shard // RING, RING), AXES)
    rows = P(AXES, None)
    flat = P(None, ("xl", "y"))
    wide = P(None, ("xl", "y"), None)
    return jax.shard_map(
        on_device,
        mesh=fine,
        in_specs=(
            rows, rows, P(), flat, flat, wide, flat, flat, wide, flat, flat, flat, wide, flat,
            wide, flat,
        ),
        out_specs=(
            rows, rows, flat, flat, wide, flat, flat, wide, flat, flat, flat, wide, flat, wide,
            flat,
        ),
        check_vma=False,
    )
```

time: 2080 us -> 797 us (0.38)
  waiting for transfers between devices: 1070 us -> 153 us
  matrix products: 454 us -> 21.9 us
  Pallas kernels: 0 us -> 330 us
  blocking collectives: 350 us -> 132 us
  local copies, waits for them, and re-layouts: 119 us -> 51 us
  starting transfers between devices: 1.57 us -> 52.1 us
    reduce_scatter x8 -> x0, waiting for transfers between devices: 605 us -> none  [the longest x2 193 us: share_grads(): lax.psum_scatter(gradients[9].astype(jnp.bfloat16), 'shard', scatter_dime...]
    dot_general x248 -> x8, matrix products: 454 us -> 21.9 us  [weight_grad(): lax.dot_general(left, right, (((0,), (0,)), ((), ())), preferred_element_...]
    all_gather x12 -> x0, waiting for transfers between devices: 357 us -> none  [the longest x2 173 us: fetch_weights(): lax.all_gather(own_part[11], 'shard', axis=0, tiled=True)]
    pallas_call x0 -> x13, Pallas kernels: none -> 330 us  [the longest x9 300 us: comm_call(): pl.pallas_call(functools.partial(comm_kernel, cfg, in_names + list(outs)...]
    all_gather x18 -> x1, blocking collectives: 253 us -> 18.7 us  [on_device(): lax.all_gather(vectors, ('xl', 'y'), axis=2, tiled=True).astype(F32)]
    psum x1, waiting for transfers between devices: 40.6 us -> 126 us  [rank_sum(): return lax.psum(value.astype(BF), ('z', 'xh', 'xl'))]
    unnamed x25 -> x1, waiting for transfers between devices: 67.2 us -> 0.02 us
    dynamic_slice x64 -> x1, local copies, waits for them, and re-layouts: 37.6 us -> 0.58 us  [on_device(): slopes = lax.dynamic_slice(slopes_all, (rank * 2,), (2,))]
  transfers between devices with their start and end apart: 23 -> 29, of which waited for: 17 -> 7; matrix products, arithmetic and copies ran while one was open for 12% -> 9% of each run, Pallas kernels for 0% -> 10%
where the time goes in v1:
time: 797 us; the launch traced here: 790 us
  Pallas kernels  330 us (41%)
  waiting for transfers between devices  153 us (19%)
  blocking collectives  132 us (17%)
  starting transfers between devices  52.1 us (7%)
  local copies, waits for them, and re-layouts  51 us (6%)
  other arithmetic  35.1 us (4%)
  matrix products  21.9 us (3%)
  between operations  15.3 us (2%)
    pallas_call x9, Pallas kernels, comm_call(): pl.pallas_call(functools.partial(comm_kernel, cfg, in_names + list(outs)...  300 us
    psum x1, waiting for transfers between devices, rank_sum(): return lax.psum(value.astype(BF), ('z', 'xh', 'xl'))  126 us
    psum x1, blocking collectives, on_device(): norms = lax.psum(jnp.stack([g['norms'] for g in grads], axis=1), AXES)  64.6 us
    psum x1, blocking collectives, rank_sum(): return lax.psum(value.astype(BF), ('z', 'xh', 'xl'))  31.1 us
    pallas_call x4, Pallas kernels, attention_call(): pl.pallas_call(kernel, out_shape=jax.ShapeDtypeStruct((qkv.shape[0], widt...  29.2 us
    dot_general x8, matrix products, weight_grad(): lax.dot_general(left, right, (((0,), (0,)), ((), ())), preferred_element_...  21.9 us
    unnamed x126, local copies, waits for them, and re-layouts  20.1 us
    all_gather x1, blocking collectives, on_device(): lax.all_gather(vectors, ('xl', 'y'), axis=2, tiled=True).astype(F32)  18.7 us
  transfers between devices with their start and end apart: 29, of which 7 were waited for; matrix products, arithmetic and copies ran while one was open for 9% of the time, Pallas kernels for 10%

profile of v1, /device:TPU:1, one launch (start us, length us, event | category | flops | bytes accessed | tf_op | source)
XLA Modules:
  0.0 789.9 jit_solution(2524889364952025272)
XLA Ops:
  19.1 5.0 all-to-all-start.2
  24.7 18.7 %all_gather.3 = bf16[6,2,1024]{2,1,0:T(2,128)(2,1)S(1)} all-gather(bf16[6,2,128]{2,1,0:T(2,128)(2,1)S(1)} %constant_dynamic-update-slice_fusion), channel_id=1, replica_groups=mesh['z'=4,'xh'=2,'c'=2,'xl'=2,'y'=4] {'xl','y'}, dimensions={2}, use_global_device_ids=true | all-gather | bytes 27648 | tf_op jit(solution)/shard_map/all_gather | solution.py:492
  64.3 3.7 all-to-all-done
  68.0 3.5 all-to-all-start.3
  86.3 6.7 all-to-all-done.1
  98.0 36.4 %shard_map.271 = (bf16[1024,1024]{1,0:T(8,128)(2,1)}, bf16[1024,384]{1,0:T(8,128)(2,1)}) custom-call(bf16[128,1024]{1,0:T(8,128)(2,1)} %refs_2_.3, f32[1,1024]{1,0:T(1,128)} %get-tuple-element.180.refs_1_.refs_3_, f32[1,1024]{1,0:T(1,128)} %get-tuple-element.179.refs_2_, bf16[1024,384]{1,0:T(8,128)(2,1)} %copy.118.refs_3_, f32[1,384]{1,0:T(1,128)} %broadcast_in_dim.6.refs_4_), custom_call_target="tpu_custom_call" | custom-call | flops 805306368 | bytes 20000000 | tf_op jit(solution)/shard_map/pallas_call | solution.py:311
  135.5 6.6 shard_map.272.refs_0_
  148.4 37.1 %shard_map.273 = (bf16[1024,128]{1,0:T(8,128)(2,1)}, f32[128,1024]{1,0:T(8,128)}, bf16[1024,1024]{1,0:T(8,128)(2,1)}, f32[1024,512]{1,0:T(8,128)}, bf16[1024,512]{1,0:T(8,128)(2,1)}) custom-call(bf16[1024,128]{1,0:T(8,128)(2,1)} %shard_map.272.refs_0_, bf16[128,1024]{1,0:T(8,128)(2,1)} %copy.122.refs_1_, bf16[128,1024]{1,0:T(8,128)(2,1)} %refs_2_.3, ...), custom_call_target="tpu_custom_call" | custom-call | flops 1342177280 | bytes 20000000 | tf_op jit(solution)/shard_map/pallas_call | solution.py:311
  191.7 34.8 %shard_map.274 = (f32[128,1024]{1,0:T(8,128)}, bf16[1024,1024]{1,0:T(8,128)(2,1)}, bf16[1024,384]{1,0:T(8,128)(2,1)}) custom-call(bf16[1024,512]{1,0:T(8,128)(2,1)} %get-tuple-element.54.refs_0_, bf16[512,1024]{1,0:T(8,128)(2,1)} %copy.129.refs_1_, f32[128,1024]{1,0:T(8,128)} %get-tuple-element.55.refs_2_, f32[1,1024]{1,0:T(1,128)} %get-tuple-element.175.refs_3_, ...), custom_call_target="tpu_custom_call" | custom-call | flops 1879048192 | bytes 20000000 | tf_op jit(solution)/shard_map/pallas_call | solution.py:311
  226.4 6.5 shard_map.275.refs_0_
  233.0 35.0 %shard_map.276 = (bf16[1024,128]{1,0:T(8,128)(2,1)}, f32[128,1024]{1,0:T(8,128)}, bf16[1024,1024]{1,0:T(8,128)(2,1)}, f32[1024,512]{1,0:T(8,128)}, bf16[1024,512]{1,0:T(8,128)(2,1)}) custom-call(bf16[1024,128]{1,0:T(8,128)(2,1)} %shard_map.275.refs_0_, bf16[128,1024]{1,0:T(8,128)(2,1)} %copy.134.refs_1_, f32[128,1024]{1,0:T(8,128)} %get-tuple-element.57.refs_2_, ...), custom_call_target="tpu_custom_call" | custom-call | flops 1342177280 | bytes 20000000 | tf_op jit(solution)/shard_map/pallas_call | solution.py:311
  268.0 31.2 %shard_map.277 = (f32[128,1024]{1,0:T(8,128)}, bf16[1024,1024]{1,0:T(8,128)(2,1)}, bf16[1024,512]{1,0:T(8,128)(2,1)}) custom-call(bf16[1024,512]{1,0:T(8,128)(2,1)} %get-tuple-element.58.refs_0_, bf16[512,1024]{1,0:T(8,128)(2,1)} %copy.137.refs_1_, f32[128,1024]{1,0:T(8,128)} %get-tuple-element.59.refs_2_, f32[1,1024]{1,0:T(1,128)} %get-tuple-element.169.refs_3_, ...), custom_call_target="tpu_custom_call" | custom-call | flops 2147483648 | bytes 20000000 | tf_op jit(solution)/shard_map/pallas_call | solution.py:311
  299.2 4.0 convolution_convert_fusion
  305.5 31.0 %shard_map.278 = (f32[128,1024]{1,0:T(8,128)}, f32[1,1024]{1,0:T(1,128)}, f32[1,1024]{1,0:T(1,128)}, bf16[1024,1024]{1,0:T(8,128)(2,1)}, bf16[1024,128]{1,0:T(8,128)(2,1)}) custom-call(bf16[1024,512]{1,0:T(8,128)(2,1)} %get-tuple-element.62.refs_0_, bf16[512,1024]{1,0:T(8,128)(2,1)} %bitcast.179, f32[128,1024]{1,0:T(8,128)} %get-tuple-element.59.refs_2_, ...), custom_call_target="tpu_custom_call" | custom-call | flops 1342177280 | bytes 20000000 | tf_op jit(solution)/shard_map/pallas_call | solution.py:311
  336.5 8.2 %shard_map.279.refs_0_ = bf16[1024,384]{1,0:T(8,128)(2,1)} custom-call(f32[2]{0:T(128)} %dynamic_slice.32.slopes, bf16[1024,384]{1,0:T(8,128)(2,1)} %get-tuple-element.56.qkv, bf16[1024,128]{1,0:T(8,128)(2,1)} %get-tuple-element.63.gctx), custom_call_target="tpu_custom_call" | custom-call | flops 4000000000 | bytes 2000000 | tf_op jit(solution)/shard_map/pallas_call | solution.py:394
  344.7 39.2 %shard_map.280 = (bf16[1024,384]{1,0:T(8,128)(2,1)}, f32[128,1024]{1,0:T(8,128)}, f32[1,1024]{1,0:T(1,128)}, f32[1,1024]{1,0:T(1,128)}, bf16[1024,1024]{1,0:T(8,128)(2,1)}, /*index=5*/bf16[1024,512]{1,0:T(8,128)(2,1)}) custom-call(bf16[1024,384]{1,0:T(8,128)(2,1)} %shard_map.279.refs_0_, bf16[384,1024]{1,0:T(8,128)(2,1)} %bitcast.189, ...), custom_call_target="tpu_custom_call" | custom-call | flops 1879048192 | bytes 20000000 | tf_op jit(solution)/shard_map/pallas_call | solution.py:311
  384.0 4.0 convolution_convert_fusion.1
  390.5 4.3 convolution_convert_fusion.3
  394.8 32.5 %shard_map.281 = (f32[128,1024]{1,0:T(8,128)}, f32[1,1024]{1,0:T(1,128)}, f32[1,1024]{1,0:T(1,128)}, bf16[1024,1024]{1,0:T(8,128)(2,1)}, bf16[1024,128]{1,0:T(8,128)(2,1)}) custom-call(bf16[1024,512]{1,0:T(8,128)(2,1)} %get-tuple-element.66.refs_0_, bf16[512,1024]{1,0:T(8,128)(2,1)} %bitcast.178, f32[128,1024]{1,0:T(8,128)} %get-tuple-element.55.refs_2_, ...), custom_call_target="tpu_custom_call" | custom-call | flops 1342177280 | bytes 20000000 | tf_op jit(solution)/shard_map/pallas_call | solution.py:311
  427.3 8.0 %shard_map.282.refs_0_ = bf16[1024,384]{1,0:T(8,128)(2,1)} custom-call(f32[2]{0:T(128)} %dynamic_slice.32.slopes, bf16[1024,384]{1,0:T(8,128)(2,1)} %get-tuple-element.53.qkv, bf16[1024,128]{1,0:T(8,128)(2,1)} %get-tuple-element.68.gctx), custom_call_target="tpu_custom_call" | custom-call | flops 4000000000 | bytes 2000000 | tf_op jit(solution)/shard_map/pallas_call | solution.py:394
  435.3 23.1 %shard_map.283 = (bf16[1024,384]{1,0:T(8,128)(2,1)}, f32[128,1024]{1,0:T(8,128)}, f32[1,1024]{1,0:T(1,128)}, f32[1,1024]{1,0:T(1,128)}) custom-call(bf16[1024,384]{1,0:T(8,128)(2,1)} %shard_map.282.refs_0_, bf16[384,1024]{1,0:T(8,128)(2,1)} %bitcast.188, bf16[128,1024]{1,0:T(8,128)(2,1)} %refs_2_.3, f32[1,1024]{1,0:T(1,128)} %get-tuple-element.180.refs_1_.refs_3_, ...), custom_call_target="tpu_custom_call" | custom-call | flops 805306368 | bytes 20000000 | tf_op jit(solution)/shard_map/pallas_call | solution.py:311
  465.7 125.8 %all-reduce.4.cloned.1.call-done = (bf16[8,128,384]{1,2,0:T(8,128)(2,1)}, bf16[8,128,384]{1,2,0:T(8,128)(2,1)}, bf16[128,1024]{0,1:T(8,128)(2,1)}, bf16[128,1024...) async-done(((bf16[8,128,384]{1,2,0:T(8,128)(2,1)}, ...) | async-done | bytes 6291472 | tf_op jit(solution)/shard_map/psum | solution.py:447
  591.5 17.2 %all_to_all.40 = bf16[8,128,384]{1,2,0:T(8,128)(2,1)} all-to-all(bf16[8,128,384]{1,2,0:T(8,128)(2,1)} %get-tuple-element.153), channel_id=1, replica_groups=mesh['z'=4,'xh'=2,'c'=2,'xl'=2,'y'=4] {'c','y'}, dimensions={0} | all-to-all | bytes 1572864 | tf_op jit(solution)/shard_map/all_to_all | solution.py:453
  608.8 3.8 all-to-all-start.4
  618.4 6.4 all-to-all-done.4
  625.6 3.8 all-to-all-start.7
  634.9 31.1 %all-reduce = (bf16[1024]{0:T(1024)(128)(2,1)S(1)}, bf16[1024]{0:T(1024)(128)(2,1)S(1)}) all-reduce(bf16[1024]{0:T(1024)(128)(2,1)S(1)} %dynamic-update-slice.4, bf16[1024]{0:T(1024)(128)(2,1)S(1)} %dynamic-update-slice.9), channel_id=1, replica_groups=mesh['z'=4,'xh'=2,'c'=2,'xl'=2,'y'=4] {'z','xh','xl'}, use_global_device_ids=true, to_apply=%region_12.13 | all-reduce | flops 2048 | bytes 8192 | tf_op jit(solution)/shard_map/psum | solution.py:447
  666.0 7.4 collective-permute-start.14
  673.6 64.6 %psum.77 = f32[4,2,1024]{2,0,1:T(4,128)S(1)} all-reduce(f32[4,2,1024]{2,0,1:T(4,128)S(1)} %pad_maximum_fusion), channel_id=1, replica_groups=mesh['z'=4,'xh'=2,'c'=2,'xl'=2,'y'=4] {'z','xh','c','xl','y'}, use_global_device_ids=true, to_apply=%region_0.1 | all-reduce | flops 8192 | bytes 65536 | tf_op jit(solution)/shard_map/psum | solution.py:596
  739.9 3.9 all-to-all-start.6
  752.3 6.4 all-to-all-done.6
  765.6 5.3 copy.150
  (264 shorter events, 119.2 us)
Async XLA Ops:
  7.2 46.6 %collective-permute-start.1 = (bf16[2,128]{1,0:T(2,128)(2,1)}, bf16[2,128]{1,0:T(2,128)(2,1)}, u32[]{:S(2)}, u32[]{:S(2)}) collective-permute-start(bf16[2,128]{1,0:T(2,128)(2,1)} %param.22), channel_id=1, source_target_pairs={{0,4},{12,8},{1,5},{13,9},{2,6},{14,10},{3,7},{15,11},{16,20},{28,... | collective-permute-start | bytes 1544 | tf_op jit(solution)/shard_map/ppermute | solution.py:437
  8.6 46.5 %collective-permute-start.2 = (bf16[2,128]{1,0:T(2,128)(2,1)}, bf16[2,128]{1,0:T(2,128)(2,1)}, u32[]{:S(2)}, u32[]{:S(2)}) collective-permute-start(bf16[2,128]{1,0:T(2,128)(2,1)} %param.23), channel_id=1, source_target_pairs={{0,4},{12,8},{1,5},{13,9},{2,6},{14,10},{3,7},{15,11},{16,20},{28,... | collective-permute-start | bytes 1544 | tf_op jit(solution)/shard_map/ppermute | solution.py:437
  9.9 48.4 %collective-permute-start.5 = (bf16[2,512]{1,0:T(2,128)(2,1)}, bf16[2,512]{1,0:T(2,128)(2,1)S(1)}, u32[]{:S(2)}, u32[]{:S(2)}) collective-permute-start(bf16[2,512]{1,0:T(2,128)(2,1)} %param.29), channel_id=1, source_target_pairs={{0,4},{12,8},{1,5},{13,9},{2,6},{14,10},{3,7},{15,11},{16,20},{28,... | collective-permute-start | bytes 6152 | tf_op jit(solution)/shard_map/ppermute | solution.py:437
  13.1 49.3 %collective-permute-start.3 = (bf16[128,1024]{0,1:T(8,128)(2,1)}, bf16[128,1024]{0,1:T(8,128)(2,1)}, u32[]{:S(2)}, u32[]{:S(2)}) collective-permute-start(bf16[128,1024]{0,1:T(8,128)(2,1)} %bitcast.15), channel_id=1, source_target_pairs={{0,4},{12,8},{1,5},{13,9},{2,6},{14,10},{3,7},{15,11},{16,20},{28,... | collective-permute-start | bytes 786440 | tf_op jit(solution)/shard_map/ppermute | solution.py:437
  15.3 56.2 %collective-permute-start.8 = (bf16[128,1024]{0,1:T(8,128)(2,1)}, bf16[128,1024]{0,1:T(8,128)(2,1)}, u32[]{:S(2)}, u32[]{:S(2)}) collective-permute-start(bf16[128,1024]{0,1:T(8,128)(2,1)} %bitcast.34), channel_id=1, source_target_pairs={{0,4},{12,8},{1,5},{13,9},{2,6},{14,10},{3,7},{15,11},{16,20},{28,... | collective-permute-start | bytes 786440 | tf_op jit(solution)/shard_map/ppermute | solution.py:437
  19.1 39.2 %all-to-all-start.2 = ((bf16[4,128,384]{1,2,0:T(8,128)(2,1)}), bf16[4,128,384]{1,2,0:T(8,128)(2,1)S(1)}, u32[]{:S(2)}, u32[]{:S(2)}) async-start(bf16[4,128,384]{1,2,0:T(8,128)(2,1)} %bitcast.31), calls=%async_computation.2 | async-start | bytes 786432 | tf_op jit(solution)/shard_map/all_to_all | solution.py:425
  53.8 131.8 %collective-permute-start.6 = (bf16[512,1024]{0,1:T(8,128)(2,1)}, bf16[512,1024]{0,1:T(8,128)(2,1)}, u32[]{:S(2)}, u32[]{:S(2)}) collective-permute-start(bf16[512,1024]{0,1:T(8,128)(2,1)} %bitcast.23), channel_id=1, source_target_pairs={{0,4},{12,8},{1,5},{13,9},{2,6},{14,10},{3,7},{15,11},{16,20},{28,... | collective-permute-start | bytes 3145736 | tf_op jit(solution)/shard_map/ppermute | solution.py:437
  55.1 133.5 %collective-permute-start.10 = (bf16[512,1024]{0,1:T(8,128)(2,1)S(1)}, bf16[512,1024]{0,1:T(8,128)(2,1)}, u32[]{:S(2)}, u32[]{:S(2)}) collective-permute-start(bf16[512,1024]{0,1:T(8,128)(2,1)S(1)} %bitcast.180), channel_id=1, source_target_pairs={{0,4},{12,8},{1,5},{13,9},{2,6},{14,10},{3,7},{15,11},{16,20},{28,... | collective-permute-start | bytes 3145736 | tf_op jit(solution)/shard_map/ppermute | solution.py:437
  58.3 9.7 %all-to-all-start = ((bf16[4,128,384]{1,2,0:T(8,128)(2,1)}), bf16[4,128,384]{1,2,0:T(8,128)(2,1)S(1)}, u32[]{:S(2)}, u32[]{:S(2)}) async-start(bf16[4,128,384]{1,2,0:T(8,128)(2,1)} %bitcast.12), calls=%async_computation | async-start | bytes 786432 | tf_op jit(solution)/shard_map/all_to_all | solution.py:425
  68.0 11.8 %all-to-all-start.3 = ((bf16[4,128,512]{1,2,0:T(8,128)(2,1)}), bf16[4,128,512]{1,2,0:T(8,128)(2,1)S(1)}, u32[]{:S(2)}, u32[]{:S(2)}) async-start(bf16[4,128,512]{1,2,0:T(8,128)(2,1)} %dynamic-slice_bitcast_fusion), calls=%async_computation.3 | async-start | bytes 1048576 | tf_op jit(solution)/shard_map/all_to_all | solution.py:425
  73.5 20.4 %collective-permute-start = (bf16[512,384]{0,1:T(8,128)(2,1)S(1)}, bf16[512,384]{0,1:T(8,128)(2,1)}, u32[]{:S(2)}, u32[]{:S(2)}) collective-permute-start(bf16[512,384]{0,1:T(8,128)(2,1)S(1)} %copy_bitcast_fusion.3), channel_id=1, source_target_pairs={{0,4},{4,0},{1,5},{5,1},{2,6},{6,2},{3,7},{7,3},{8,12},{12,8},{9,1... | collective-permute-start | bytes 1179656 | tf_op jit(solution)/shard_map/ppermute | solution.py:427
  79.8 13.1 %all-to-all-start.1 = ((bf16[4,128,512]{1,2,0:T(8,128)(2,1)}), bf16[4,128,512]{1,2,0:T(8,128)(2,1)S(1)}, u32[]{:S(2)}, u32[]{:S(2)}) async-start(bf16[4,128,512]{1,2,0:T(8,128)(2,1)} %dynamic-slice_bitcast_fusion.1), calls=%async_computation.1 | async-start | bytes 1048576 | tf_op jit(solution)/shard_map/all_to_all | solution.py:425
  83.3 508.2 %all-reduce.4.cloned.1.call-start = ((), (), s32[]{:S(2)}) async-start(), calls=%async_computation.8 | async-start | bytes 12582912 | tf_op jit(solution)/shard_map/psum | solution.py:447
  84.2 12.4 %collective-permute-start.7 = (bf16[512,384]{0,1:T(8,128)(2,1)}, bf16[512,384]{0,1:T(8,128)(2,1)S(1)}, u32[]{:S(2)}, u32[]{:S(2)}) collective-permute-start(bf16[512,384]{0,1:T(8,128)(2,1)} %copy_bitcast_fusion.2), channel_id=1, source_target_pairs={{0,4},{4,0},{1,5},{5,1},{2,6},{6,2},{3,7},{7,3},{8,12},{12,8},{9,1... | collective-permute-start | bytes 1179656 | tf_op jit(solution)/shard_map/ppermute | solution.py:427
  86.2 55.9 %collective-permute-start.9 = (bf16[512,512]{0,1:T(8,128)(2,1)S(1)}, bf16[512,512]{0,1:T(8,128)(2,1)}, u32[]{:S(2)}, u32[]{:S(2)}) collective-permute-start(bf16[512,512]{0,1:T(8,128)(2,1)S(1)} %copy_bitcast_fusion), channel_id=1, source_target_pairs={{0,4},{4,0},{1,5},{5,1},{2,6},{6,2},{3,7},{7,3},{8,12},{12,8},{9,1... | collective-permute-start | bytes 1572872 | tf_op jit(solution)/shard_map/ppermute | solution.py:427
  93.8 51.4 %collective-permute-start.4 = (bf16[512,512]{0,1:T(8,128)(2,1)}, bf16[512,512]{0,1:T(8,128)(2,1)}, u32[]{:S(2)}, u32[]{:S(2)}) collective-permute-start(bf16[512,512]{0,1:T(8,128)(2,1)} %copy_bitcast_fusion.1), channel_id=1, source_target_pairs={{0,4},{4,0},{1,5},{5,1},{2,6},{6,2},{3,7},{7,3},{8,12},{12,8},{9,1... | collective-permute-start | bytes 1572872 | tf_op jit(solution)/shard_map/ppermute | solution.py:427
  608.8 16.0 %all-to-all-start.4 = ((bf16[8,128,384]{1,2,0:T(8,128)(2,1)}), bf16[8,128,384]{1,2,0:T(8,128)(2,1)S(1)}, u32[]{:S(2)}, u32[]{:S(2)}) async-start(bf16[8,128,384]{1,2,0:T(8,128)(2,1)} %get-tuple-element.154), calls=%async_computation.4 | async-start | bytes 1572864 | tf_op jit(solution)/shard_map/all_to_all | solution.py:453
  616.8 56.7 %copy-start.25 = (f32[1,1024]{1,0:T(1,128)S(1)}, f32[1,1024]{1,0:T(1,128)}, u32[]{:S(2)}) copy-start(f32[1,1024]{1,0:T(1,128)} %get-tuple-element.77) | copy-start | bytes 12292
  625.6 114.3 %all-to-all-start.7 = ((bf16[8,128,512]{2,1,0:T(8,128)(2,1)}), bf16[8,128,512]{2,1,0:T(8,128)(2,1)S(1)}, u32[]{:S(2)}, u32[]{:S(2)}) async-start(bf16[8,128,512]{2,1,0:T(8,128)(2,1)} %get-tuple-element.157), calls=%async_computation.7 | async-start | bytes 2097152 | tf_op jit(solution)/shard_map/all_to_all | solution.py:453
  629.5 114.5 %copy-start.23 = (bf16[128,1024]{0,1:T(8,128)(2,1)S(1)}, bf16[128,1024]{0,1:T(8,128)(2,1)}, u32[]{:S(2)}) copy-start(bf16[128,1024]{0,1:T(8,128)(2,1)} %get-tuple-element.156) | copy-start | bytes 786436
  630.3 115.4 %copy-start.24 = (bf16[128,1024]{0,1:T(8,128)(2,1)S(1)}, bf16[128,1024]{0,1:T(8,128)(2,1)}, u32[]{:S(2)}) copy-start(bf16[128,1024]{0,1:T(8,128)(2,1)} %get-tuple-element.155) | copy-start | bytes 786436
  666.0 72.9 %collective-permute-start.14 = (bf16[1024]{0:T(1024)(128)(2,1)S(1)}, bf16[1024]{0:T(1024)(128)(2,1)S(1)}, u32[]{:S(2)}, u32[]{:S(2)}) collective-permute-start(bf16[1024]{0:T(1024)(128)(2,1)S(1)} %get-tuple-element.151), channel_id=1, source_target_pairs={{0,8},{8,0},{1,9},{9,1},{2,10},{10,2},{3,11},{11,3},{4,12},{12,4},... | collective-permute-start | bytes 6152 | tf_op jit(solution)/shard_map/ppermute | solution.py:442
  673.4 70.4 %collective-permute-start.13 = (bf16[1024]{0:T(1024)(128)(2,1)S(1)}, bf16[1024]{0:T(1024)(128)(2,1)S(1)}, u32[]{:S(2)}, u32[]{:S(2)}) collective-permute-start(bf16[1024]{0:T(1024)(128)(2,1)S(1)} %get-tuple-element.152), channel_id=1, source_target_pairs={{0,8},{8,0},{1,9},{9,1},{2,10},{10,2},{3,11},{11,3},{4,12},{12,4},... | collective-permute-start | bytes 6152 | tf_op jit(solution)/shard_map/ppermute | solution.py:442
  738.9 6.8 collective-permute-start.16
  739.8 20.5 %collective-permute-start.20 = (bf16[512,1024]{0,1:T(8,128)(2,1)}, bf16[512,1024]{0,1:T(8,128)(2,1)}, u32[]{:S(2)}, u32[]{:S(2)}) collective-permute-start(bf16[512,1024]{0,1:T(8,128)(2,1)} %get-tuple-element.159), channel_id=1, source_target_pairs={{0,8},{8,0},{1,9},{9,1},{2,10},{10,2},{3,11},{11,3},{4,12},{12,4},... | collective-permute-start | bytes 3145736 | tf_op jit(solution)/shard_map/ppermute | solution.py:442
  739.9 18.9 %all-to-all-start.6 = ((bf16[8,128,512]{2,1,0:T(8,128)(2,1)}), bf16[8,128,512]{2,1,0:T(8,128)(2,1)S(1)}, u32[]{:S(2)}, u32[]{:S(2)}) async-start(bf16[8,128,512]{2,1,0:T(8,128)(2,1)} %get-tuple-element.158), calls=%async_computation.6 | async-start | bytes 2097152 | tf_op jit(solution)/shard_map/all_to_all | solution.py:453
  743.8 18.1 %collective-permute-start.19 = (bf16[512,1024]{0,1:T(8,128)(2,1)}, bf16[512,1024]{0,1:T(8,128)(2,1)}, u32[]{:S(2)}, u32[]{:S(2)}) collective-permute-start(bf16[512,1024]{0,1:T(8,128)(2,1)} %get-tuple-element.160), channel_id=1, source_target_pairs={{0,8},{8,0},{1,9},{9,1},{2,10},{10,2},{3,11},{11,3},{4,12},{12,4},... | collective-permute-start | bytes 3145736 | tf_op jit(solution)/shard_map/ppermute | solution.py:442
  744.0 2.9 collective-permute-start.15
  750.7 20.3 %collective-permute-start.11 = (bf16[128,3072]{0,1:T(8,128)(2,1)}, bf16[128,3072]{0,1:T(8,128)(2,1)}, u32[]{:S(2)}, u32[]{:S(2)}) collective-permute-start(bf16[128,3072]{0,1:T(8,128)(2,1)} %bitcast.59), channel_id=1, source_target_pairs={{0,8},{8,0},{1,9},{9,1},{2,10},{10,2},{3,11},{11,3},{4,12},{12,4},... | collective-permute-start | bytes 2359304 | tf_op jit(solution)/shard_map/ppermute | solution.py:442
  750.8 21.6 %collective-permute-start.12 = (bf16[128,3072]{0,1:T(8,128)(2,1)S(1)}, bf16[128,3072]{0,1:T(8,128)(2,1)}, u32[]{:S(2)}, u32[]{:S(2)}) collective-permute-start(bf16[128,3072]{0,1:T(8,128)(2,1)S(1)} %bitcast.185), channel_id=1, source_target_pairs={{0,8},{8,0},{1,9},{9,1},{2,10},{10,2},{3,11},{11,3},{4,12},{12,4},... | collective-permute-start | bytes 2359304 | tf_op jit(solution)/shard_map/ppermute | solution.py:442
  759.9 16.3 %collective-permute-start.17 = (bf16[128,4096]{1,0:T(8,128)(2,1)}, bf16[128,4096]{1,0:T(8,128)(2,1)}, u32[]{:S(2)}, u32[]{:S(2)}) collective-permute-start(bf16[128,4096]{1,0:T(8,128)(2,1)} %bitcast.99), channel_id=1, source_target_pairs={{0,8},{8,0},{1,9},{9,1},{2,10},{10,2},{3,11},{11,3},{4,12},{12,4},... | collective-permute-start | bytes 3145736 | tf_op jit(solution)/shard_map/ppermute | solution.py:442
  760.3 17.3 %collective-permute-start.18 = (bf16[128,4096]{1,0:T(8,128)(2,1)}, bf16[128,4096]{1,0:T(8,128)(2,1)}, u32[]{:S(2)}, u32[]{:S(2)}) collective-permute-start(bf16[128,4096]{1,0:T(8,128)(2,1)} %bitcast.103), channel_id=1, source_target_pairs={{0,8},{8,0},{1,9},{9,1},{2,10},{10,2},{3,11},{11,3},{4,12},{12,4},... | collective-permute-start | bytes 3145736 | tf_op jit(solution)/shard_map/ppermute | solution.py:442
  (47 other events, 806.0 us)
Sparse Core Ops, SparseCore 0:
  465.8 125.6 all-reduce.3

commit v2 on v1

v2 whole, which is shorter than its diff:
```python
import functools
from types import SimpleNamespace

import jax
import jax.numpy as jnp
from jax import lax
from jax.experimental import pallas as pl
from jax.experimental.pallas import tpu as pltpu
from jax.sharding import Mesh
from jax.sharding import PartitionSpec as P

eps = 1e-05
MESH = pl.DeviceIdType.MESH
AXES = ("z", "xh", "c", "xl", "y")
BF = jnp.bfloat16
F32 = jnp.float32
BLK = 128
HALF = 64
WIDTH = 1024
RING = 4
CALL_VMEM = 56 * 1024 * 1024


def gelu(u):
    t = jnp.tanh(0.7978845608028654 * (u + 0.044715 * u * u * u))
    return 0.5 * u * (1.0 + t)


def gelu_slope(u):
    sq = u * u
    t = jnp.tanh(0.7978845608028654 * (u + 0.044715 * sq * u))
    return 0.5 * (1.0 + t) + 0.5 * u * (1.0 - t * t) * (
        0.7978845608028654 * (1.0 + 3.0 * 0.044715 * sq)
    )


def norm_parts(values):
    average = jnp.mean(values, axis=-1, keepdims=True)
    centred = values - average
    variance = jnp.mean(centred * centred, axis=-1, keepdims=True)
    r = lax.rsqrt(variance + eps)
    return centred * r, r


def comm_kernel(cfg, names, *refs):
    ref = SimpleNamespace(**dict(zip(names, refs)))
    env = neighbours()
    z, c, xl, y = env.z, env.c, env.xl, env.y
    up, down, far = lax.rem(y + 1, RING), lax.rem(y + 3, RING), lax.rem(y + 2, RING)
    oc, ox = 1 - c, 1 - xl
    sib, nxt, prv, xnb = {"c": oc}, {"y": up}, {"y": down}, {"xl": ox}
    shard, rank = xl * RING + y, c * RING + y
    if cfg.ship:
        plane = [
            (lax.rem(xl + dx, 2), lax.rem(y + dy, RING))
            for dx, dy in ((0, 2), (1, 2), (1, 1), (1, 3), (0, 1), (0, 3), (1, 0))
        ]
        peers = [{"xl": px, "y": py} for px, py in plane]
        z_far = {"z": lax.rem(z + 2, RING)}
        partners = [sib] + peers + [env.z_next, env.z_prev, z_far]
    else:
        partners = [sib, nxt, prv] + ([xnb] if cfg.swap_in or cfg.swap_out else [])

    if cfg.reduce:
        partners = partners + env.reduce_partners
    enter(partners)

    sent = []

    def push(src, dst, target):
        i = len(sent)
        copy = pltpu.make_async_remote_copy(
            src_ref=src,
            dst_ref=dst,
            send_sem=ref.send.at[i],
            recv_sem=ref.recv.at[i],
            device_id=target,
            device_id_type=MESH,
        )
        copy.start()
        sent.append(copy)
        return copy

    local = []
    stored = [0]

    def store(src, dst):
        copy = pltpu.make_async_copy(src, dst, ref.local.at[stored[0]])
        copy.start()
        stored[0] += 1
        local.append(copy)

    def rows(group, q, offset=0, size=BLK):
        return pl.ds(pl.multiple_of((group * RING + q) * BLK + offset, HALF), size)

    def ship_columns(raw, layer, dst, parts):
        per = dst.shape[3] // parts
        quarter = pl.ds(pl.multiple_of(z * dst.shape[2], dst.shape[2]), dst.shape[2])
        copies, keeps = [], []
        for j in range(parts):
            for (_, py), peer in zip(plane, peers):
                cols = pl.ds(pl.multiple_of((j * 2 * RING + c * RING + py) * per, per), per)
                copies.append(
                    push(raw.at[layer, quarter, cols], dst.at[shard, z, :, pl.ds(j * per, per)], peer)
                )
            cols = pl.ds(pl.multiple_of((j * 2 * RING + rank) * per, per), per)
            store(raw.at[layer, quarter, cols], dst.at[shard, z, :, pl.ds(j * per, per)])
            keeps.append(local.pop())
        return dst, copies, keeps

    def ship_quarters(step):
        dst, copies, keeps = step
        for copy in copies:
            copy.wait_recv()
        for copy in keeps:
            copy.wait()
        view = dst.at[:, z]
        return [push(view, view, target) for target in (env.z_next, env.z_prev, z_far)]

    shipped_rows = []

    def ship_rows(raw, layer, dst):
        i = len(shipped_rows)
        copy = pltpu.make_async_remote_copy(
            src_ref=raw.at[layer],
            dst_ref=dst,
            send_sem=ref.row_send.at[i],
            recv_sem=ref.row_recv.at[i],
            device_id=xnb,
            device_id_type=MESH,
        )
        keep = pltpu.make_async_copy(raw.at[layer], dst, ref.row_local.at[i])
        shipped_rows.append((copy, keep))

        @pl.when(c == xl)
        def _():
            copy.start()
            keep.start()

    def ship_rows_wait():
        for copy, keep in shipped_rows:

            @pl.when(c == xl)
            def _():
                copy.wait_send()
                keep.wait()

            @pl.when(c != xl)
            def _():
                copy.wait_recv()

    shipped = []

    def ship_all():
        for kind, name, layer, parts in cfg.ship:
            if kind == "cols":
                dst = getattr(ref, "w_" + name)
                shipped.append(ship_columns(getattr(ref, "raw_" + name), layer, dst, parts))
            else:
                ship_rows(getattr(ref, "raw_" + name), layer, getattr(ref, "w_" + name))

    def gather_start(block):
        own = rows(c, y)
        low, high = rows(c, y, 0, HALF), rows(c, y, HALF, HALF)
        gbuf = ref.gbuf
        gbuf[own, :] = block
        first = [
            push(gbuf.at[low], gbuf.at[low], nxt),
            push(gbuf.at[high], gbuf.at[high], prv),
            push(gbuf.at[own], gbuf.at[own], sib),
            push(gbuf.at[high], gbuf.at[high], nxt),
            push(gbuf.at[low], gbuf.at[low], prv),
        ]
        return first

    def gather_rest(first, consume):
        gbuf = ref.gbuf
        low_n, high_p, own_s, high_n, low_p = first
        consume(c, y)
        low_n.wait_recv()
        part = gbuf.at[rows(c, down, 0, HALF)]
        fwd_n = push(part, part, nxt)
        high_p.wait_recv()
        part = gbuf.at[rows(c, up, HALF, HALF)]
        fwd_p = push(part, part, prv)
        own_s.wait_recv()
        consume(oc, y)
        high_n.wait_recv()
        part = gbuf.at[rows(c, down)]
        sib_a = push(part, part, sib)
        low_p.wait_recv()
        part = gbuf.at[rows(c, up)]
        sib_b = push(part, part, sib)
        consume(c, down)
        consume(c, up)
        advance(jobs, 1)
        sib_a.wait_recv()
        consume(oc, down)
        sib_b.wait_recv()
        consume(oc, up)
        fwd_n.wait_recv()
        fwd_p.wait_recv()
        part = gbuf.at[rows(c, far)]
        sib_c = push(part, part, sib)
        consume(c, far)
        sib_c.wait_recv()
        consume(oc, far)

    if cfg.mid == "ln":
        vec = ref.vec
        pack_copies = [push(ref.pack, vec.at[shard], peer) for peer in peers]
        vec[shard] = ref.pack[...]
        first_weights = ship_columns(ref.raw_first, 0, ref.w_first, 3)
        for copy in pack_copies:
            copy.wait_recv()
        ref.vec_out[...] = vec[...]

        def full_vector(row):
            return jnp.concatenate(
                [vec[s, row : row + 1, :] for s in range(2 * RING)], axis=1
            ).astype(F32)

    ship_all()
    arriving = []
    jobs, job_sent, reduced = [], [], []
    if cfg.reduce:
        bufs = [getattr(ref, name) for name in REDUCE_NAMES]
        half = len(bufs) // 2
        jobs = [
            reduce_job(env, True, 0, ref.grads, ref.totals, bufs[:half], job_sent, reduced),
            reduce_job(env, False, 1, ref.grads, ref.totals, bufs[half:], job_sent, reduced),
        ]
        advance(jobs, 1)

    first = None
    if cfg.mid == "fin":
        first = gather_start(ref.grad_out[...])

    acc = None
    if cfg.rs:
        order = [far, up, down, y]
        lhs = ref.lhs
        chunks = []
        if cfg.swap_in:
            rowbuf = ref.rowbuf
            for q in order:
                chunks.append(push(lhs.at[rows(ox, q)], rowbuf.at[rows(xl, q)], xnb))
            mine = pl.ds(pl.multiple_of(xl * RING * BLK, BLK), RING * BLK)
            rowbuf[mine, :] = lhs[mine, :]
        else:
            rowbuf = lhs

        def partial(group, q):
            return jnp.dot(
                rowbuf[rows(group, q), :], ref.w_rs[...], preferred_element_type=F32
            )

        own, sib_out, sib_in = ref.own, ref.sib_out, ref.sib_in
        stage = ref.stage
        near_n, near_p, far_n, far_p = ref.near_n, ref.near_p, ref.far_n, ref.far_p
        low, high = pl.ds(0, HALF), pl.ds(HALF, HALF)
        ring = SimpleNamespace()
        passed = []

        def begin(slot):
            if chunks:
                chunks[slot].wait_recv()
            sib_out[slot] = partial(oc, order[slot]).astype(BF)
            passed.append(push(sib_out.at[slot], sib_in.at[slot], sib))
            own[slot] = partial(c, order[slot])

        def finish(slot):
            passed[slot].wait_recv()
            total = own[slot] + sib_in[slot].astype(F32)
            if slot == 0:
                stage[0] = total.astype(BF)
                ring.fn = push(stage.at[0, low], far_n, nxt)
                ring.fp = push(stage.at[0, high], far_p, prv)
            elif slot == 1:
                stage[1, high, :] = total[HALF:].astype(BF)
                ring.nh = push(stage.at[1, high], near_n.at[high], nxt)
                own[1, low, :] = total[:HALF]
            elif slot == 2:
                stage[2, low, :] = total[:HALF].astype(BF)
                ring.pl = push(stage.at[2, low], near_p.at[low], prv)
                own[2, high, :] = total[HALF:]
            else:
                own[3] = total

        begin(0)
        begin(1)
        finish(0)
        begin(2)
        finish(1)
        begin(3)
        finish(2)
        ring.fn.wait_recv()
        stage[1, low, :] = (own[1, low, :] + far_n[...].astype(F32)).astype(BF)
        ring.nl = push(stage.at[1, low], near_n.at[low], nxt)
        ring.fp.wait_recv()
        stage[2, high, :] = (own[2, high, :] + far_p[...].astype(F32)).astype(BF)
        ring.ph = push(stage.at[2, high], near_p.at[high], prv)
        finish(3)
        advance(jobs, 2)
        if cfg.swap_in:
            store(rowbuf, ref.rows_out)
        for copy in (ring.nh, ring.pl, ring.nl, ring.ph):
            copy.wait_recv()
        acc = own[3] + near_n[...].astype(F32) + near_p[...].astype(F32)

    block = None
    if cfg.mid == "ln":
        xhat, _ = norm_parts(ref.resid[...].astype(F32))
        block = (xhat * full_vector(0) + full_vector(2)).astype(BF)
    elif cfg.mid == "fwd":
        hidden = ref.resid[...].astype(F32) + (acc + ref.bias_rs[...])
        ref.hidden[...] = hidden
        xhat, _ = norm_parts(hidden)
        block = (xhat * ref.gain[...] + ref.shift[...]).astype(BF)
    elif cfg.mid == "fin":
        ref.hidden[...] = ref.resid[...].astype(F32) + (acc + ref.bias_rs[...])
    elif cfg.mid == "bwd":
        xhat, r = norm_parts(ref.resid[...].astype(F32))
        ref.g_gain[...] = jnp.sum(acc * xhat, axis=0, keepdims=True)
        ref.g_shift[...] = jnp.sum(acc, axis=0, keepdims=True)
        scaled = acc * ref.gain[...]
        grad = ref.stream[...].astype(F32) + r * (
            scaled
            - jnp.mean(scaled, axis=-1, keepdims=True)
            - xhat * jnp.mean(scaled * xhat, axis=-1, keepdims=True)
        )
        ref.hidden[...] = grad
        block = grad.astype(BF)

    if cfg.tail is not None:
        if first is None:
            first = gather_start(block)
        if cfg.mid == "ln":
            quarters = ship_quarters(first_weights)
            arriving.extend(copy for step in shipped for copy in ship_quarters(step))
            for copy in quarters:
                copy.wait_recv()
            store(ref.w_first, ref.w_qkv_first)
            weights = ref.w_first[...].reshape(WIDTH, 3 * BLK)
            q_row, v_row = vec[rank, 12:13, :].astype(F32), vec[rank, 14:15, :].astype(F32)
            bias_tail = jnp.concatenate([q_row, jnp.zeros_like(q_row), v_row], axis=1)
        else:
            arriving.extend(copy for step in shipped for copy in ship_quarters(step))
            weights = ref.w_ag
            bias_tail = ref.bias_ag[...] if hasattr(ref, "bias_ag") else None
        done = {}
        out_copies = []

        def consume(group, q):
            where = rows(group, q)
            value = jnp.dot(ref.gbuf[where, :], weights[...], preferred_element_type=F32)
            if cfg.tail == "up":
                pre = value + bias_tail
                ref.pre[where, :] = pre
                ref.active[where, :] = gelu(pre).astype(BF)
            elif cfg.tail == "dpre":
                ref.grad_pre[where, :] = (value * gelu_slope(ref.pre_in[where, :])).astype(BF)
            else:
                if cfg.tail == "qkv":
                    value = value + bias_tail
                pbuf, xbuf = ref.pbuf, ref.xbuf
                pbuf[where, :] = value.astype(BF)
                key = id(q)
                done[key] = done.get(key, 0) + 1
                if done[key] == 2:
                    out_copies.append(push(pbuf.at[rows(ox, q)], xbuf.at[rows(xl, q)], xnb))
                    xbuf[rows(xl, q), :] = pbuf[rows(xl, q), :]

        gather_rest(first, consume)
        store(ref.gbuf, ref.gathered)
        if cfg.swap_out:
            for copy in out_copies:
                copy.wait_recv()
            ref.att[...] = ref.xbuf[...]
    for copy in arriving:
        copy.wait_recv()
    if cfg.reduce:
        run_jobs(jobs)
        for copy in reduced:
            copy.wait()
    ship_rows_wait()
    for copy in sent + job_sent:
        copy.wait_send()
    for copy in local:
        copy.wait()


RANK_WIDTHS = dict(qkv=(8, 4, 32, 384), up=(8, 4, 32, 512), dense=(128, 1024), down=(512, 1024))


def comm_call(
    cid, *, mid, rs=False, swap_in=False, tail=None, ship=(), reduce=False, **operands
):
    swap_out = tail in ("qkv", "gctx")
    cfg = SimpleNamespace(
        rs=rs, swap_in=swap_in, swap_out=swap_out, mid=mid, tail=tail, ship=ship,
        reduce=reduce,
    )
    whole = pl.BlockSpec(memory_space=pltpu.VMEM)
    in_names = list(operands)
    operands = SimpleNamespace(**operands)
    total_rows = 2 * RING * BLK
    outs = SimpleNamespace()
    scratch = SimpleNamespace()
    flops = 0
    if rs:
        k = operands.lhs.shape[1]
        flops += 2 * total_rows * k * WIDTH
        if swap_in:
            outs.rows_out = ((total_rows, k), BF, pl.ANY)
            scratch.rowbuf = pltpu.VMEM((total_rows, k), BF)
        scratch.own = pltpu.VMEM((RING, BLK, WIDTH), F32)
        scratch.sib_out = pltpu.VMEM((RING, BLK, WIDTH), BF)
        scratch.sib_in = pltpu.VMEM((RING, BLK, WIDTH), BF)
        scratch.stage = pltpu.VMEM((3, BLK, WIDTH), BF)
        scratch.near_n = pltpu.VMEM((BLK, WIDTH), BF)
        scratch.near_p = pltpu.VMEM((BLK, WIDTH), BF)
        scratch.far_n = pltpu.VMEM((HALF, WIDTH), BF)
        scratch.far_p = pltpu.VMEM((HALF, WIDTH), BF)
    for kind, name, _, _ in ship:
        setattr(outs, "w_" + name, (RANK_WIDTHS[name], BF, pl.ANY))
    if mid == "ln":
        outs.w_qkv_first = (RANK_WIDTHS["qkv"], BF, pl.ANY)
        outs.vec_out = ((2 * RING,) + operands.pack.shape, BF, pltpu.VMEM)
        scratch.vec = pltpu.VMEM((2 * RING,) + operands.pack.shape, BF)
        scratch.w_first = pltpu.VMEM(RANK_WIDTHS["qkv"], BF)
    else:
        outs.hidden = ((BLK, WIDTH), F32, pltpu.VMEM)
    if mid == "bwd":
        outs.g_gain = ((1, WIDTH), F32, pltpu.VMEM)
        outs.g_shift = ((1, WIDTH), F32, pltpu.VMEM)
    if tail is not None:
        n = 3 * BLK if mid == "ln" else operands.w_ag.shape[1]
        flops += 2 * total_rows * n * WIDTH
        outs.gathered = ((total_rows, WIDTH), BF, pl.ANY)
        scratch.gbuf = pltpu.VMEM((total_rows, WIDTH), BF)
        if tail == "up":
            outs.pre = ((total_rows, n), F32, pltpu.VMEM)
            outs.active = ((total_rows, n), BF, pltpu.VMEM)
        elif tail == "dpre":
            outs.grad_pre = ((total_rows, n), BF, pltpu.VMEM)
        else:
            outs.att = ((total_rows, n), BF, pltpu.VMEM)
            scratch.pbuf = pltpu.VMEM((total_rows, n), BF)
            scratch.xbuf = pltpu.VMEM((total_rows, n), BF)
    if reduce:
        outs.totals = (operands.grads.shape, BF, pl.ANY)
        for name, shape in zip(REDUCE_NAMES, reduce_scratch() * 2):
            setattr(scratch, name, shape)
    scratch.send = pltpu.SemaphoreType.DMA((80 if ship else 32,))
    scratch.recv = pltpu.SemaphoreType.DMA((80 if ship else 32,))
    scratch.local = pltpu.SemaphoreType.DMA((12,))
    if ship:
        scratch.row_send = pltpu.SemaphoreType.DMA((2,))
        scratch.row_recv = pltpu.SemaphoreType.DMA((2,))
        scratch.row_local = pltpu.SemaphoreType.DMA((2,))
    results = pl.pallas_call(
        functools.partial(comm_kernel, cfg, in_names + list(vars(outs)) + list(vars(scratch))),
        out_shape=[jax.ShapeDtypeStruct(shape, dtype) for shape, dtype, _ in vars(outs).values()],
        in_specs=[
            pl.BlockSpec(memory_space=pl.ANY) if name.startswith("raw_") else whole
            for name in in_names
        ],
        out_specs=[pl.BlockSpec(memory_space=space) for _, _, space in vars(outs).values()],
        scratch_shapes=list(vars(scratch).values()),
        cost_estimate=pl.CostEstimate(flops=flops, bytes_accessed=20_000_000, transcendentals=0),
        compiler_params=pltpu.CompilerParams(
            collective_id=cid, has_side_effects=True, vmem_limit_bytes=CALL_VMEM
        ),
    )(*vars(operands).values())
    result = SimpleNamespace(**dict(zip(vars(outs), results)))
    for name in ("w_qkv", "w_up", "w_qkv_first"):
        if hasattr(result, name):
            weight = getattr(result, name)
            setattr(result, name, weight.reshape(WIDTH, weight.shape[3]))
    return result


QB = 256


def head_only(values, head):
    lane = lax.broadcasted_iota(jnp.int32, values.shape, 1)
    keep = (lane // 64) == head
    return jnp.where(keep, values, jnp.zeros_like(values))


def probs_of(q_pad, keys, slope, start):
    count = keys.shape[0]
    scores = lax.dot_general(
        keys, q_pad, (((1,), (1,)), ((), ())), preferred_element_type=F32
    )
    key_pos = lax.broadcasted_iota(jnp.int32, (count, QB), 0)
    query_pos = lax.broadcasted_iota(jnp.int32, (count, QB), 1) + start
    scores = scores + slope * key_pos.astype(F32)
    scores = jnp.where(key_pos <= query_pos, scores, -1000000000.0)
    top = jnp.max(scores, axis=0, keepdims=True)
    exponent = jnp.exp(scores - top)
    total = jnp.sum(exponent, axis=0, keepdims=True)
    return exponent * (1.0 / total)


def attention_fwd_kernel(slopes, qkv, ctx):
    value_t = qkv[:, 2 * BLK : 3 * BLK].astype(F32).T.astype(BF)
    for start in range(0, qkv.shape[0], QB):
        count = start + QB
        queries = qkv[start : start + QB, 0:BLK] * jnp.asarray(0.125, BF)
        keys = qkv[0:count, BLK : 2 * BLK]
        parts = []
        for head in range(2):
            probs = probs_of(head_only(queries, head), keys, slopes[head], start).astype(BF)
            ctx_t = jnp.dot(value_t[:, 0:count], probs, preferred_element_type=F32)
            parts.append(ctx_t[head * 64 : head * 64 + 64])
        ctx[start : start + QB, :] = jnp.concatenate(parts, axis=0).T.astype(BF)


def attention_bwd_kernel(slopes, qkv, gctx, dqkv, dk, dv):
    key_t = qkv[:, BLK : 2 * BLK].astype(F32).T.astype(BF)
    dk[...] = jnp.zeros_like(dk)
    dv[...] = jnp.zeros_like(dv)
    for start in range(0, qkv.shape[0], QB):
        count = start + QB
        queries = qkv[start : start + QB, 0:BLK] * jnp.asarray(0.125, BF)
        keys = qkv[0:count, BLK : 2 * BLK]
        values = qkv[0:count, 2 * BLK : 3 * BLK]
        grads = gctx[start : start + QB, :]
        parts = []
        for head in range(2):
            q_pad = head_only(queries, head)
            g_pad = head_only(grads, head)
            probs = probs_of(q_pad, keys, slopes[head], start)
            grad_probs = lax.dot_general(
                values, g_pad, (((1,), (1,)), ((), ())), preferred_element_type=F32
            )
            inner = jnp.sum(probs * grad_probs, axis=0, keepdims=True)
            grad_scores = (probs * (grad_probs - inner)).astype(BF)
            dk[0:count, :] += jnp.dot(grad_scores, q_pad, preferred_element_type=F32)
            dv[0:count, :] += jnp.dot(probs.astype(BF), g_pad, preferred_element_type=F32)
            dq_t = jnp.dot(key_t[:, 0:count], grad_scores, preferred_element_type=F32)
            parts.append(dq_t[head * 64 : head * 64 + 64] * 0.125)
        dqkv[start : start + QB, 0:BLK] = jnp.concatenate(parts, axis=0).T.astype(BF)
    dqkv[:, BLK : 2 * BLK] = dk[...].astype(BF)
    dqkv[:, 2 * BLK : 3 * BLK] = dv[...].astype(BF)


def attention_call(kernel, slopes, qkv, *more, width, scratch=()):
    whole = pl.BlockSpec(memory_space=pltpu.VMEM)
    return pl.pallas_call(
        kernel,
        out_shape=jax.ShapeDtypeStruct((qkv.shape[0], width), BF),
        in_specs=[pl.BlockSpec(memory_space=pltpu.SMEM), whole] + [whole] * len(more),
        out_specs=whole,
        scratch_shapes=list(scratch),
        cost_estimate=pl.CostEstimate(
            flops=4_000_000_000, bytes_accessed=2_000_000, transcendentals=2_000_000
        ),
        compiler_params=pltpu.CompilerParams(vmem_limit_bytes=CALL_VMEM),
    )(slopes, qkv, *more)


def attention_forward(slopes, qkv):
    return attention_call(attention_fwd_kernel, slopes, qkv, width=BLK)


def attention_backward(slopes, qkv, gctx):
    scratch = [pltpu.VMEM((qkv.shape[0], BLK), F32)] * 2
    return attention_call(
        attention_bwd_kernel, slopes, qkv, gctx, width=3 * BLK, scratch=scratch
    )


PIECE = 208
COLS = 512
LANES = 256


def neighbours():
    z, xh, c, xl, y = (lax.axis_index(name) for name in AXES)
    x = xh * 2 + xl

    def at_x(value):
        value = lax.rem(value, RING)
        return {"xh": value // 2, "xl": lax.rem(value, 2)}

    env = SimpleNamespace(z=z, xh=xh, c=c, xl=xl, y=y, x=x)
    env.x_next, env.x_prev = at_x(x + 1), at_x(x + 3)
    env.z_next, env.z_prev = {"z": lax.rem(z + 1, RING)}, {"z": lax.rem(z + 3, RING)}
    env.across, env.diagonal, env.sib = {"xh": 1 - xh}, {"xl": 1 - xl, "c": 1 - c}, {"c": 1 - c}
    env.mates = [(1 - c, y)]
    for dy in (2, 1, 3):
        env.mates += [(c, lax.rem(y + dy, RING)), (1 - c, lax.rem(y + dy, RING))]
    env.reduce_partners = [env.x_next, env.x_prev, env.z_next, env.z_prev, env.across, env.diagonal]
    env.reduce_partners += [{"c": core, "y": other} for core, other in env.mates]
    return env


def enter(partners):
    barrier = pltpu.get_barrier_semaphore()
    for partner in partners:
        pl.semaphore_signal(barrier, inc=1, device_id=partner, device_id_type=MESH)
    pl.semaphore_wait(barrier, len(partners))


def advance(jobs, steps):
    for _ in range(steps):
        for one in list(jobs):
            if next(one, 1) == 1:
                jobs.remove(one)


def run_jobs(jobs):
    while jobs:
        advance(jobs, 1)


def reduce_job(env, x_first, half, grads, out, bufs, sent, local):
    (far_n, far_p, near_n, near_p, stage_n, stage_p, total, far2_n, far2_p, near2_n, near2_p,
     stage2_n, stage2_p, summed, final_piece, final, send, recv, keep) = bufs
    c, xl, x, z = env.c, env.xl, env.x, env.z
    rank = c * RING + env.y
    lanes = pl.ds(half * LANES, LANES)
    count = [0]

    def push(src, dst, target):
        i = count[0]
        count[0] += 1
        copy = pltpu.make_async_remote_copy(
            src_ref=src, dst_ref=dst, send_sem=send.at[i], recv_sem=recv.at[i],
            device_id=target, device_id_type=MESH,
        )
        copy.start()
        sent.append(copy)
        return copy

    a, b = (x, z) if x_first else (z, x)
    a_next, a_prev = (env.x_next, env.x_prev) if x_first else (env.z_next, env.z_prev)
    b_next, b_prev = (env.z_next, env.z_prev) if x_first else (env.x_next, env.x_prev)

    def piece(index, start, size):
        if x_first:
            return grads.at[index, pl.ds(start, size), :, lanes]
        return grads.at[pl.ds(start, size), index, :, lanes]

    def load(view):
        return view[...].astype(F32)

    far, up, down = (lax.rem(a + d, RING) for d in (2, 1, 3))
    lo, hi = pl.ds(0, 2), pl.ds(2, 2)
    fn = push(piece(far, 0, 2), far_n, a_next)
    fp = push(piece(far, 2, 2), far_p, a_prev)
    nh = push(piece(up, 2, 2), near_n.at[hi], a_next)
    pl_ = push(piece(down, 0, 2), near_p.at[lo], a_prev)
    yield 0
    fn.wait_recv()
    stage_n[...] = (load(piece(up, 0, 2)) + far_n[...].astype(F32)).astype(BF)
    nl = push(stage_n, near_n.at[lo], a_next)
    fp.wait_recv()
    stage_p[...] = (load(piece(down, 2, 2)) + far_p[...].astype(F32)).astype(BF)
    ph = push(stage_p, near_p.at[hi], a_prev)
    yield 0
    yield 0
    for copy in (nh, pl_, nl, ph):
        copy.wait_recv()
    for q in range(RING):
        own = load(piece(a, q, 1))
        total[q] = (
            own.reshape(PIECE, LANES) + near_n[q].astype(F32) + near_p[q].astype(F32)
        ).astype(BF)

    far, up, down = (lax.rem(b + d, RING) for d in (2, 1, 3))
    cut = 96
    lo, hi = pl.ds(0, cut), pl.ds(cut, PIECE - cut)
    fn = push(total.at[far, lo], far2_n, b_next)
    fp = push(total.at[far, hi], far2_p, b_prev)
    nh = push(total.at[up, hi], near2_n.at[hi], b_next)
    pl_ = push(total.at[down, lo], near2_p.at[lo], b_prev)
    yield 0
    fn.wait_recv()
    stage2_n[...] = (total[up, lo, :].astype(F32) + far2_n[...].astype(F32)).astype(BF)
    nl = push(stage2_n, near2_n.at[lo], b_next)
    fp.wait_recv()
    stage2_p[...] = (total[down, hi, :].astype(F32) + far2_p[...].astype(F32)).astype(BF)
    ph = push(stage2_p, near2_p.at[hi], b_prev)
    yield 0
    for copy in (nh, pl_, nl, ph):
        copy.wait_recv()
    summed[...] = (
        total[b].astype(F32) + near2_n[...].astype(F32) + near2_p[...].astype(F32)
    ).astype(BF)

    def slot(number):
        return pl.ds(pl.multiple_of(number * 16, 16), 16)

    copies = [
        push(
            summed.at[slot(core * RING + other)], final_piece.at[slot(rank)],
            {"c": core, "y": other},
        )
        for core, other in env.mates
    ]
    final_piece[slot(rank), :] = summed[slot(rank), :]
    final_piece[2 * RING * 16 :, :] = summed[2 * RING * 16 :, :]
    yield 0
    for copy in copies:
        copy.wait_recv()

    trade = pltpu.make_async_remote_copy(
        src_ref=final_piece, dst_ref=final.at[x, z], send_sem=keep.at[0],
        recv_sem=keep.at[1], device_id=env.diagonal, device_id_type=MESH,
    )

    @pl.when(c != xl)
    def _():
        trade.start()

    @pl.when(c == xl)
    def _():
        final[x, z] = final_piece[...]

    yield 0

    @pl.when(c != xl)
    def _():
        trade.wait()

    mine, other = env.xh * 2 + c, (1 - env.xh) * 2 + c
    zn, zp, zf = (lax.rem(z + d, RING) for d in (1, 3, 2))

    def spread(first, second, target):
        view = final.at[first, second]
        return push(view, view, target)

    one_n = spread(mine, z, env.z_next)
    cross = spread(mine, z, env.across)
    one_p = spread(mine, z, env.z_prev)
    siblings = [spread(mine, z, env.sib)]
    yield 0
    cross.wait_recv()
    two_p = spread(other, z, env.z_prev)
    two_n = spread(other, z, env.z_next)
    siblings.append(spread(other, z, env.sib))
    yield 0
    one_n.wait_recv()
    fwd_n = spread(mine, zp, env.z_next)
    siblings.append(spread(mine, zp, env.sib))
    two_p.wait_recv()
    fwd_p = spread(other, zn, env.z_prev)
    siblings.append(spread(other, zn, env.sib))
    yield 0
    one_p.wait_recv()
    siblings.append(spread(mine, zn, env.sib))
    two_n.wait_recv()
    siblings.append(spread(other, zp, env.sib))
    yield 0
    fwd_n.wait_recv()
    siblings.append(spread(mine, zf, env.sib))
    fwd_p.wait_recv()
    siblings.append(spread(other, zf, env.sib))
    yield 0
    for copy in siblings:
        copy.wait_recv()
    back = pltpu.make_async_copy(final, out.at[:, :, :, lanes], keep.at[2])
    back.start()
    local.append(back)


def reduce_scratch():
    two, four = (2, PIECE, LANES), (4, PIECE, LANES)
    one, low, high = (PIECE, LANES), (96, LANES), (PIECE - 96, LANES)
    shapes = [two, two, four, four, two, two, four, low, high, one, one, low, high, one, one]
    return [pltpu.VMEM(shape, BF) for shape in shapes] + [
        pltpu.VMEM((RING, RING, PIECE, LANES), BF),
        pltpu.SemaphoreType.DMA((40,)),
        pltpu.SemaphoreType.DMA((40,)),
        pltpu.SemaphoreType.DMA((3,)),
    ]


REDUCE_NAMES = ["job%d" % i for i in range(38)]


def reduce_kernel(grads, out, *bufs):
    env = neighbours()
    enter(env.reduce_partners)
    sent, local = [], []
    half = len(bufs) // 2
    run_jobs(
        [
            reduce_job(env, True, 0, grads, out, bufs[:half], sent, local),
            reduce_job(env, False, 1, grads, out, bufs[half:], sent, local),
        ]
    )
    for copy in sent:
        copy.wait_send()
    for copy in local:
        copy.wait()


def reduce_call(cid, grads):
    return pl.pallas_call(
        reduce_kernel,
        out_shape=jax.ShapeDtypeStruct(grads.shape, BF),
        in_specs=[pl.BlockSpec(memory_space=pltpu.VMEM)],
        out_specs=pl.BlockSpec(memory_space=pl.ANY),
        scratch_shapes=reduce_scratch() * 2,
        compiler_params=pltpu.CompilerParams(
            collective_id=cid, has_side_effects=True, vmem_limit_bytes=CALL_VMEM
        ),
    )(grads)


def grads_kernel(input_a, dproj, input_b, grad_pre, context, grad_attn, active, grad_mlp, norms, out):
    rank = lax.axis_index("c") * RING + lax.axis_index("y")

    def product(left, right):
        return lax.dot_general(
            left, right, (((0,), (0,)), ((), ())), preferred_element_type=F32
        ).astype(BF)

    def column_sums(values):
        return jnp.sum(values.astype(F32), axis=0, keepdims=True)

    here = pl.ds(pl.multiple_of(rank * BLK, BLK), BLK)
    sums_p, sums_u = column_sums(dproj[...]), column_sums(grad_pre[...])
    rows = [sums_p[:, :BLK], sums_p[:, 2 * BLK :]]
    rows += [column_sums(grad_attn[:, here]), column_sums(grad_mlp[:, here])]
    rows += [sums_u[:, i * BLK : (i + 1) * BLK] for i in range(4)]
    vectors = jnp.concatenate(rows, axis=0)
    empty = jnp.zeros((16, BLK), BF)
    for t in range(2 * RING):
        cols = slice(t * BLK, (t + 1) * BLK)
        g_qkv = product(input_a[:, cols], dproj[...])
        g_up = product(input_b[:, cols], grad_pre[...])
        spare = jnp.concatenate(
            [jnp.where(rank == t, vectors, jnp.zeros_like(vectors)), norms[:, cols],
             jnp.zeros((4, BLK), F32)],
            axis=0,
        ).astype(BF)
        slot = slice(t * 16, t * 16 + 16)
        for i in range(8):
            x, zr = i // 2, i % 2
            part = slice(i * 16, i * 16 + 16)
            out[x, zr * 2, slot, 0:384] = g_qkv[part]
            out[x, zr * 2, slot, 384:512] = g_up[part, 0:128]
            out[x, zr * 2 + 1, slot, 0:384] = g_up[part, 128:512]
            out[x, zr * 2 + 1, slot, 384:512] = spare if i == 0 else empty
    g_dense = product(context[...], grad_attn[...])
    for i in range(8):
        x, zr = i // 2, i % 2
        g_down = product(active[:, i * 64 : i * 64 + 64], grad_mlp[...])
        for zc in range(2):
            lanes = slice(zc * COLS, zc * COLS + COLS)
            out[x, zr * 2 + zc, 128:144, :] = g_dense[i * 16 : i * 16 + 16, lanes]
            out[x, zr * 2 + zc, 144:208, :] = g_down[:, lanes]


def grads_call(*operands):
    whole = pl.BlockSpec(memory_space=pltpu.VMEM)
    return pl.pallas_call(
        grads_kernel,
        out_shape=jax.ShapeDtypeStruct((RING, RING, PIECE, COLS), BF),
        in_specs=[whole] * len(operands),
        out_specs=whole,
        compiler_params=pltpu.CompilerParams(vmem_limit_bytes=CALL_VMEM),
    )(*operands)


def unpack_kernel(final0, final1, qkv, up, dense, down, spare):
    layer, x = pl.program_id(0), pl.program_id(1)

    def write(final):
        for zr in range(2):
            rows = slice(zr * 16, zr * 16 + 16)
            for k in range(2 * RING):
                slot = slice(k * 16, k * 16 + 16)
                left = final[0, zr * 2, slot, :].astype(F32)
                right = final[0, zr * 2 + 1, slot, :].astype(F32)
                for j in range(3):
                    at = j * WIDTH + k * BLK
                    qkv[0, rows, at : at + BLK] = left[:, j * BLK : (j + 1) * BLK]
                up[0, rows, k * 512 : k * 512 + 128] = left[:, 384:512]
                up[0, rows, k * 512 + 128 : k * 512 + 512] = right[:, 0:384]
            for zc in range(2):
                lanes = slice(zc * COLS, zc * COLS + COLS)
                dense[0, rows, lanes] = final[0, zr * 2 + zc, 128:144, :].astype(F32)
                down[0, zr * 64 : zr * 64 + 64, lanes] = final[0, zr * 2 + zc, 144:208, :].astype(F32)

        @pl.when(x == 0)
        def _():
            total = final[0, 1, 0:16, 384:512].astype(F32)
            for k in range(1, 2 * RING):
                total = total + final[0, 1, k * 16 : k * 16 + 16, 384:512].astype(F32)
            spare[0] = total

    @pl.when(layer == 0)
    def _():
        write(final0)

    @pl.when(layer == 1)
    def _():
        write(final1)


def unpack_call(final0, final1):
    layers = 2

    def block(index):
        def at(layer, x):
            return (jnp.where(layer == index, x, (RING - 1) * (1 - index)), 0, 0, 0)

        return pl.BlockSpec((1, RING, PIECE, COLS), at)

    def rows(count, width):
        return pl.BlockSpec((1, count, width), lambda layer, x: (layer, x, 0))

    return pl.pallas_call(
        unpack_kernel,
        grid=(layers, RING),
        out_shape=[
            jax.ShapeDtypeStruct((layers, BLK, 3 * WIDTH), F32),
            jax.ShapeDtypeStruct((layers, BLK, 4 * WIDTH), F32),
            jax.ShapeDtypeStruct((layers, BLK, WIDTH), F32),
            jax.ShapeDtypeStruct((layers, 4 * BLK, WIDTH), F32),
            jax.ShapeDtypeStruct((layers, 16, BLK), F32),
        ],
        in_specs=[block(0), block(1)],
        out_specs=[
            rows(32, 3 * WIDTH), rows(32, 4 * WIDTH), rows(32, WIDTH), rows(128, WIDTH),
            pl.BlockSpec((1, 16, BLK), lambda layer, x: (layer, 0, 0)),
        ],
        compiler_params=pltpu.CompilerParams(vmem_limit_bytes=CALL_VMEM),
    )(final0, final1)


def on_device(
    tokens,
    grad_out,
    slope_index,
    ln1_gain,
    ln1_bias,
    qkv_weight,
    q_bias,
    v_bias,
    dense_weight,
    dense_bias,
    ln2_gain,
    ln2_bias,
    up_weight,
    up_bias,
    down_weight,
    down_bias,
):
    layers = qkv_weight.shape[0]
    heads = slope_index.shape[0]
    rank = lax.axis_index("c") * RING + lax.axis_index("y")
    slopes_all = jnp.exp2(-8.0 * (slope_index.astype(F32) + 1.0) / heads)
    slopes = lax.dynamic_slice(slopes_all, (rank * 2,), (2,))

    pack = jnp.concatenate(
        [ln1_gain, ln1_bias, dense_bias, ln2_gain, ln2_bias, down_bias, q_bias, v_bias]
        + [up_bias.reshape(8, BLK), jnp.zeros((8, BLK), BF)]
    )
    step = comm_call(
        1, mid="ln", tail="qkv", resid=tokens, pack=pack, raw_first=qkv_weight,
        raw_up=up_weight, raw_dense=dense_weight,
        ship=(("cols", "up", 0, 1), ("rows", "dense", 0, 0)),
    )
    gathered = step.vec_out.astype(F32)
    ranked = lax.dynamic_index_in_dim(gathered, rank, 0, keepdims=False)
    gathered = gathered.transpose(1, 0, 2).reshape(gathered.shape[1], WIDTH)
    w_qkv, w_up, w_dense, w_down = [step.w_qkv_first], [step.w_up], [step.w_dense], []

    def vector(number, i):
        return gathered[number * layers + i][None, :]

    def bias_qkv(i):
        return jnp.concatenate([ranked[12 + i], jnp.zeros_like(ranked[0]), ranked[14 + i]])[None, :]

    def bias_up(i):
        return ranked[16 + 4 * i : 20 + 4 * i].reshape(1, 512)

    streams, mids, saved = [tokens], [], []
    output = None
    for i in range(layers):
        keep = SimpleNamespace(input_a=step.gathered, qkv=step.att)
        context = attention_forward(slopes, step.att)
        extra = {}
        if i == 0:
            extra = dict(
                ship=(("cols", "qkv", 1, 3), ("rows", "down", 0, 0)),
                raw_qkv=qkv_weight, raw_down=down_weight,
            )
        step = comm_call(
            2 + i, mid="fwd", rs=True, swap_in=True, tail="up", lhs=context, w_rs=w_dense[i],
            resid=streams[i], bias_rs=vector(2, i), gain=vector(3, i), shift=vector(4, i),
            w_ag=w_up[i], bias_ag=bias_up(i), **extra,
        )
        if i == 0:
            w_qkv.append(step.w_qkv)
            w_down.append(step.w_down)
        mids.append(step.hidden)
        vars(keep).update(
            context=step.rows_out, input_b=step.gathered, pre=step.pre,
            active=step.active,
        )
        saved.append(keep)
        if i + 1 < layers:
            step = comm_call(
                4, mid="fwd", rs=True, tail="qkv", lhs=step.active, w_rs=w_down[i],
                resid=mids[i], bias_rs=vector(5, i), gain=vector(0, i + 1),
                shift=vector(1, i + 1), w_ag=w_qkv[i + 1], bias_ag=bias_qkv(i + 1),
                ship=(("cols", "up", 1, 1), ("rows", "dense", 1, 0), ("rows", "down", 1, 0)),
                raw_up=up_weight, raw_dense=dense_weight, raw_down=down_weight,
            )
            w_up.append(step.w_up)
            w_dense.append(step.w_dense)
            w_down.append(step.w_down)
            streams.append(step.hidden)
        else:
            step = comm_call(
                5, mid="fin", rs=True, tail="dpre", lhs=step.active, w_rs=w_down[i],
                resid=mids[i], bias_rs=vector(5, i), grad_out=grad_out,
                w_ag=w_down[i].T, pre_in=keep.pre,
            )
            output = step.hidden

    grad_stream = grad_out
    packed = [None] * layers
    for i in reversed(range(layers)):
        keep = saved[i]
        grad_mlp, grad_pre = step.gathered, step.grad_pre
        extra = {} if i else dict(reduce=True, grads=packed[1])
        step = comm_call(
            7 - i, mid="bwd", rs=True, tail="gctx", lhs=grad_pre, w_rs=w_up[i].T,
            resid=mids[i], gain=vector(3, i), stream=grad_stream, w_ag=w_dense[i].T, **extra,
        )
        grad_after, grad_attn = step.hidden, step.gathered
        gain_b, shift_b = step.g_gain, step.g_shift
        if i == 0:
            final1 = step.totals
        dqkv = attention_backward(slopes, keep.qkv, step.att)
        if i:
            step = comm_call(
                8, mid="bwd", rs=True, swap_in=True, tail="dpre", lhs=dqkv, w_rs=w_qkv[i].T,
                resid=streams[i], gain=vector(0, i), stream=grad_after,
                w_ag=w_down[i - 1].T, pre_in=saved[i - 1].pre,
            )
        else:
            step = comm_call(
                9, mid="bwd", rs=True, swap_in=True, lhs=dqkv, w_rs=w_qkv[i].T,
                resid=streams[i], gain=vector(0, i), stream=grad_after,
            )
        grad_stream = step.hidden
        packed[i] = grads_call(
            keep.input_a, step.rows_out, keep.input_b, grad_pre, keep.context, grad_attn,
            keep.active, grad_mlp,
            jnp.concatenate([step.g_gain, step.g_shift, gain_b, shift_b]),
        )
    final0 = reduce_call(10, packed[0])
    g_qkv, g_up, g_dense, g_down, spare = unpack_call(final0, final1)
    return (
        output,
        grad_stream,
        spare[:, 8],
        spare[:, 9],
        g_qkv,
        spare[:, 0],
        spare[:, 1],
        g_dense,
        spare[:, 2],
        spare[:, 10],
        spare[:, 11],
        g_up,
        spare[:, 4:8].reshape(layers, -1),
        g_down,
        spare[:, 3],
    )


def solution(mesh):
    replica, shard = mesh.devices.shape
    fine = Mesh(mesh.devices.reshape(replica // 4, 2, 2, shard // RING, RING), AXES)
    rows = P(AXES, None)
    flat = P(None, ("xl", "y"))
    wide = P(None, ("xl", "y"), None)
    return jax.shard_map(
        on_device,
        mesh=fine,
        in_specs=(
            rows, rows, P(), flat, flat, wide, flat, flat, wide, flat, flat, flat, wide, flat,
            wide, flat,
        ),
        out_specs=(
            rows, rows, flat, flat, wide, flat, flat, wide, flat, flat, flat, wide, flat, wide,
            flat,
        ),
        check_vma=False,
    )
```

time: 797 us -> 515 us (0.65)
  waiting for transfers between devices: 153 us -> 0 us
  Pallas kernels: 330 us -> 480 us
  blocking collectives: 132 us -> 0 us
  starting transfers between devices: 52.1 us -> 0 us
  other arithmetic: 35.1 us -> 4.15 us
  local copies, waits for them, and re-layouts: 51 us -> 22.7 us
  matrix products: 21.9 us -> 0 us
  between operations: 15.3 us -> 1.12 us
    pallas_call x9 -> x13, Pallas kernels: 300 us -> 451 us  [the longest x9 362 us: comm_call(): pl.pallas_call(functools.partial(comm_kernel, cfg, in_names + list(vars(o...]
    psum x1 -> x0, waiting for transfers between devices: 126 us -> none  [rank_sum(): return lax.psum(value.astype(BF), ('z', 'xh', 'xl'))]
    psum x2 -> x0, blocking collectives: 95.8 us -> none  [the longest x1 64.6 us: on_device(): norms = lax.psum(jnp.stack([g['norms'] for g in grads], axis=1), AXES)]
    all_to_all x7 -> x0, starting transfers between devices: 27 us -> none  [the longest x4 15.4 us: columns_to_rank(): mine = lax.all_to_all(split, 'y', 0, 0, tiled=True)]
    all_to_all x7 -> x0, waiting for transfers between devices: 26.2 us -> none  [the longest x4 13.3 us: columns_to_rank(): mine = lax.all_to_all(split, 'y', 0, 0, tiled=True)]
    ppermute x21 -> x0, starting transfers between devices: 25.1 us -> none  [the longest x10 10.4 us: rank_to_shard(): other = lax.ppermute(value, 'c', [(0, 1), (1, 0)])]
    dot_general x8 -> x0, matrix products: 21.9 us -> none  [weight_grad(): lax.dot_general(left, right, (((0,), (0,)), ((), ())), preferred_element_...]
    all_gather x1 -> x0, blocking collectives: 18.7 us -> none  [on_device(): lax.all_gather(vectors, ('xl', 'y'), axis=2, tiled=True).astype(F32)]
  transfers between devices with their start and end apart: 29 -> 0, of which waited for: 7 -> 0; matrix products, arithmetic and copies ran while one was open for 9% -> 0% of each run, Pallas kernels for 10% -> 0%
where the time goes in v2:
time: 515 us; the launch traced here: 508 us
  Pallas kernels  480 us (93%)
  local copies, waits for them, and re-layouts  22.7 us (4%)
    pallas_call x9, Pallas kernels, comm_call(): pl.pallas_call(functools.partial(comm_kernel, cfg, in_names + list(vars(o...  362 us
    pallas_call x1, Pallas kernels, reduce_call(): pl.pallas_call(reduce_kernel, out_shape=jax.ShapeDtypeStruct(grads.shape,...  55.1 us
    pallas_call x4, Pallas kernels, attention_call(): pl.pallas_call(kernel, out_shape=jax.ShapeDtypeStruct((qkv.shape[0], widt...  29.1 us
    pallas_call x2, Pallas kernels, grads_call(): pl.pallas_call(grads_kernel, out_shape=jax.ShapeDtypeStruct((RING, RING,...  24.2 us

profile of v2, /device:TPU:1, one launch (start us, length us, event | category | flops | bytes accessed | tf_op | source)
XLA Modules:
  0.0 508.0 jit_solution(11456101994891915895)
XLA Ops:
  2.6 3.8 concatenate.12.refs_1_
  6.4 38.0 %shard_map.271 = (bf16[8,4,32,512]{3,2,1,0:T(8,128)(2,1)}, bf16[128,1024]{1,0:T(8,128)(2,1)}, bf16[8,4,32,384]{3,2,1,0:T(8,128)(2,1)}, bf16[8,32,128]{2,1,0:T(8,...) custom-call(bf16[128,1024]{1,0:T(8,128)(2,1)} %refs_2_.5, bf16[32,128]{1,0:T(8,128)(2,1)} %concatenate.12.refs_1_, ...), custom_call_target="tpu_custom_call" | custom-call | flops 805306368 | bytes 20000000 | tf_op jit(solution)/shard_map/pallas_call | solution.py:462
  44.4 0.9 fusion.2
  47.1 6.6 %shard_map.272.refs_0_ = bf16[1024,128]{1,0:T(8,128)(2,1)} custom-call(f32[2]{0:T(128)} %dynamic_slice.7.slopes, bf16[1024,384]{1,0:T(8,128)(2,1)} %get-tuple-element.68.qkv), custom_call_target="tpu_custom_call" | custom-call | flops 4000000000 | bytes 2000000 | tf_op jit(solution)/shard_map/pallas_call | solution.py:553
  53.8 0.9 copy.48
  54.6 1.2 copy.49
  55.8 1.8 copy.47
  57.6 49.4 %shard_map.273 = (bf16[1024,128]{1,0:T(8,128)(2,1)}, bf16[8,4,32,384]{3,2,1,0:T(8,128)(2,1)}, bf16[512,1024]{1,0:T(8,128)(2,1)}, f32[128,1024]{1,0:T(8,128)}, bf...) custom-call(bf16[1024,128]{1,0:T(8,128)(2,1)} %shard_map.272.refs_0_, ...), custom_call_target="tpu_custom_call" | custom-call | flops 1342177280 | bytes 20000000 | tf_op jit(solution)/shard_map/pallas_call | solution.py:462
  107.0 2.4 copy.45
  109.4 1.5 copy.46
  110.9 40.2 %shard_map.274 = (bf16[8,4,32,512]{3,2,1,0:T(8,128)(2,1)}, bf16[128,1024]{1,0:T(8,128)(2,1)}, bf16[512,1024]{1,0:T(8,128)(2,1)}, f32[128,1024]{1,0:T(8,128)}, bf...) custom-call(bf16[1024,512]{1,0:T(8,128)(2,1)} %get-tuple-element.72.refs_0_.active, ...), custom_call_target="tpu_custom_call" | custom-call | flops 1879048192 | bytes 20000000 | tf_op jit(solution)/shard_map/pallas_call | solution.py:462
  151.1 6.6 %shard_map.275.refs_0_ = bf16[1024,128]{1,0:T(8,128)(2,1)} custom-call(f32[2]{0:T(128)} %dynamic_slice.7.slopes, bf16[1024,384]{1,0:T(8,128)(2,1)} %get-tuple-element.76.qkv), custom_call_target="tpu_custom_call" | custom-call | flops 4000000000 | bytes 2000000 | tf_op jit(solution)/shard_map/pallas_call | solution.py:553
  157.7 0.8 copy.44
  158.5 1.3 copy.43
  159.8 1.5 copy.42
  161.3 43.8 %shard_map.276 = (bf16[1024,128]{1,0:T(8,128)(2,1)}, f32[128,1024]{1,0:T(8,128)}, bf16[1024,1024]{1,0:T(8,128)(2,1)}, f32[1024,512]{1,0:T(8,128)}, bf16[1024,512]{1,0:T(8,128)(2,1)}) custom-call(bf16[1024,128]{1,0:T(8,128)(2,1)} %shard_map.275.refs_0_, bf16[128,1024]{1,0:T(8,128)(2,1)} %get-tuple-element.77.refs_1_, f32[128,1024]{1,0:T(8,128)} %get-tuple-element.78.refs_2_, ...), custom_call_target="tpu_custom_call" | custom-call | flops 1342177280 | bytes 20000000 | tf_op jit(solution)/shard_map/pallas_call | solution.py:462
  205.1 31.4 %shard_map.277 = (f32[128,1024]{1,0:T(8,128)}, bf16[1024,1024]{1,0:T(8,128)(2,1)}, bf16[1024,512]{1,0:T(8,128)(2,1)}) custom-call(bf16[1024,512]{1,0:T(8,128)(2,1)} %get-tuple-element.80.refs_0_.active, bf16[512,1024]{1,0:T(8,128)(2,1)} %get-tuple-element.81.refs_1_, f32[128,1024]{1,0:T(8,128)} %get-tuple-element.82.refs_2_, ...), custom_call_target="tpu_custom_call" | custom-call | flops 2147483648 | bytes 20000000 | tf_op jit(solution)/shard_map/pallas_call | solution.py:462
  236.6 31.9 %shard_map.278 = (f32[128,1024]{1,0:T(8,128)}, f32[1,1024]{1,0:T(1,128)}, f32[1,1024]{1,0:T(1,128)}, bf16[1024,1024]{1,0:T(8,128)(2,1)}, bf16[1024,128]{1,0:T(8,128)(2,1)}) custom-call(bf16[1024,512]{1,0:T(8,128)(2,1)} %get-tuple-element.85.refs_0_.grad_pre, bf16[512,1024]{1,0:T(8,128)(2,1)} %bitcast.62, f32[128,1024]{1,0:T(8,128)} %get-tuple-element.82.refs_2_, ...), custom_call_target="tpu_custom_call" | custom-call | flops 1342177280 | bytes 20000000 | tf_op jit(solution)/shard_map/pallas_call | solution.py:462
  268.5 8.0 %shard_map.279.refs_0_ = bf16[1024,384]{1,0:T(8,128)(2,1)} custom-call(f32[2]{0:T(128)} %dynamic_slice.7.slopes, bf16[1024,384]{1,0:T(8,128)(2,1)} %get-tuple-element.76.qkv, bf16[1024,128]{1,0:T(8,128)(2,1)} %get-tuple-element.86.gctx), custom_call_target="tpu_custom_call" | custom-call | flops 4000000000 | bytes 2000000 | tf_op jit(solution)/shard_map/pallas_call | solution.py:553
  276.4 39.0 %shard_map.280 = (bf16[1024,384]{1,0:T(8,128)(2,1)}, f32[128,1024]{1,0:T(8,128)}, f32[1,1024]{1,0:T(1,128)}, f32[1,1024]{1,0:T(1,128)}, bf16[1024,1024]{1,0:T(8,128)(2,1)}, /*index=5*/bf16[1024,512]{1,0:T(8,128)(2,1)}) custom-call(bf16[1024,384]{1,0:T(8,128)(2,1)} %shard_map.279.refs_0_, bf16[384,1024]{1,0:T(8,128)(2,1)} %bitcast.67, ...), custom_call_target="tpu_custom_call" | custom-call | flops 1879048192 | bytes 20000000 | tf_op jit(solution)/shard_map/pallas_call | solution.py:462
  315.4 1.3 pad_maximum_fusion.norms
  316.8 12.1 %shard_map.281.refs_6_ = bf16[4,4,208,512]{3,2,1,0:T(8,128)(2,1)} custom-call(bf16[1024,1024]{1,0:T(8,128)(2,1)} %get-tuple-element.91.input_a, bf16[1024,384]{1,0:T(8,128)(2,1)} %get-tuple-element.92.dproj, bf16[1024,1024]{1,0:T(8,128)(2,1)} %get-tuple-element.93.input_b, bf16[1024,512]{1,0:T(8,128)(2,1)} %get-tuple-element.85.refs_0_.grad_pre, ...), custom_call_target="tpu_custom_call" | custom-call | tf_op jit(solution)/shard_map/pallas_call | solution.py:864
  328.8 65.6 %shard_map.282 = (f32[128,1024]{1,0:T(8,128)}, f32[1,1024]{1,0:T(1,128)}, f32[1,1024]{1,0:T(1,128)}, bf16[1024,1024]{1,0:T(8,128)(2,1)}, bf16[1024,128]{1,0:T(8,128)(2,1)}, /*index=5*/bf16[4,4,208,512]{3,2,1,0:T(8,128)(2,1)}) custom-call(bf16[1024,512]{1,0:T(8,128)(2,1)} %get-tuple-element.89.refs_0_.grad_pre, bf16[512,1024]{1,0:T(8,128)(2,1)} %bitcast.55, ...), custom_call_target="tpu_custom_call" | custom-call | flops 1342177280 | bytes 20000000 | tf_op jit(solution)/shard_map/pallas_call | solution.py:462
  394.4 8.0 %shard_map.283.refs_0_ = bf16[1024,384]{1,0:T(8,128)(2,1)} custom-call(f32[2]{0:T(128)} %dynamic_slice.7.slopes, bf16[1024,384]{1,0:T(8,128)(2,1)} %get-tuple-element.68.qkv, bf16[1024,128]{1,0:T(8,128)(2,1)} %get-tuple-element.101.gctx), custom_call_target="tpu_custom_call" | custom-call | flops 4000000000 | bytes 2000000 | tf_op jit(solution)/shard_map/pallas_call | solution.py:553
  402.4 22.7 %shard_map.284 = (bf16[1024,384]{1,0:T(8,128)(2,1)}, f32[128,1024]{1,0:T(8,128)}, f32[1,1024]{1,0:T(1,128)}, f32[1,1024]{1,0:T(1,128)}) custom-call(bf16[1024,384]{1,0:T(8,128)(2,1)} %shard_map.283.refs_0_, bf16[384,1024]{1,0:T(8,128)(2,1)} %bitcast.66, bf16[128,1024]{1,0:T(8,128)(2,1)} %refs_2_.5, f32[1,1024]{1,0:T(1,128)} %get-tuple-element.121.refs_3_, ...), custom_call_target="tpu_custom_call" | custom-call | flops 805306368 | bytes 20000000 | tf_op jit(solution)/shard_map/pallas_call | solution.py:462
  425.1 1.3 pad_maximum_fusion.1.norms
  426.4 12.1 %shard_map.285.grads = bf16[4,4,208,512]{3,2,1,0:T(8,128)(2,1)} custom-call(bf16[1024,1024]{1,0:T(8,128)(2,1)} %get-tuple-element.105.input_a, bf16[1024,384]{1,0:T(8,128)(2,1)} %get-tuple-element.106.dproj, bf16[1024,1024]{1,0:T(8,128)(2,1)} %get-tuple-element.107.input_b, bf16[1024,512]{1,0:T(8,128)(2,1)} %get-tuple-element.89.refs_0_.grad_pre, ...), custom_call_target="tpu_custom_call" | custom-call | tf_op jit(solution)/shard_map/pallas_call | solution.py:864
  438.5 55.1 %shard_map.286.final0 = bf16[4,4,208,512]{3,2,1,0:T(8,128)(2,1)} custom-call(bf16[4,4,208,512]{3,2,1,0:T(8,128)(2,1)} %shard_map.285.grads), custom_call_target="tpu_custom_call" | custom-call | tf_op jit(solution)/shard_map/pallas_call | solution.py:805
  493.6 9.8 %shard_map.287 = (f32[2,128,3072]{2,1,0:T(8,128)}, f32[2,128,4096]{2,1,0:T(8,128)}, f32[2,128,1024]{2,1,0:T(8,128)}, f32[2,512,1024]{2,1,0:T(8,128)}, f32[2,16,128]{2,1,0:T(8,128)}) custom-call(bf16[4,4,208,512]{3,2,1,0:T(8,128)(2,1)} %shard_map.286.final0, bf16[4,4,208,512]{3,2,1,0:T(8,128)(2,1)} %get-tuple-element.115.final1), custom_call_target="tpu_custom_call" | custom-call | tf_op jit(solution)/shard_map/pallas_call | solution.py:921
  504.1 1.5 fusion.3
  506.1 0.8 copy.55
  506.9 0.8 copy.56
  (38 shorter events, 5.2 us)
Async XLA Ops:
  47.1 6.6 %copy-start.2 = (bf16[128,1024]{1,0:T(8,128)(2,1)S(1)}, bf16[128,1024]{1,0:T(8,128)(2,1)}, u32[]{:S(2)}) copy-start(bf16[128,1024]{1,0:T(8,128)(2,1)} %get-tuple-element.69.refs_1_) | copy-start | bytes 786436
  47.1 7.5 %copy-start.5 = (bf16[8,4,32,384]{3,2,1,0:T(8,128)(2,1)S(1)}, bf16[8,4,32,384]{3,2,1,0:T(8,128)(2,1)}, u32[]{:S(2)}) copy-start(bf16[8,4,32,384]{3,2,1,0:T(8,128)(2,1)} %get-tuple-element.102) | copy-start | bytes 2359300
  53.8 2.0 copy-start.1
  107.0 2.4 copy-start
  151.0 6.6 %copy-start.8 = (bf16[128,1024]{1,0:T(8,128)(2,1)S(1)}, bf16[128,1024]{1,0:T(8,128)(2,1)}, u32[]{:S(2)}) copy-start(bf16[128,1024]{1,0:T(8,128)(2,1)} %get-tuple-element.77.refs_1_) | copy-start | bytes 786436
  151.1 7.5 %copy-start.4 = (bf16[8,4,32,512]{3,2,1,0:T(8,128)(2,1)S(1)}, bf16[8,4,32,512]{3,2,1,0:T(8,128)(2,1)}, u32[]{:S(2)}) copy-start(bf16[8,4,32,512]{3,2,1,0:T(8,128)(2,1)} %get-tuple-element.79) | copy-start | bytes 3145732
  157.7 2.2 copy-start.3
  276.4 39.0 %copy-start.9 = (f32[1,1024]{1,0:T(1,128)S(1)}, f32[1,1024]{1,0:T(1,128)}, u32[]{:S(2)}) copy-start(f32[1,1024]{1,0:T(1,128)} %get-tuple-element.99) | copy-start | bytes 12292
  276.4 39.0 %copy-start.10 = (f32[1,1024]{1,0:T(1,128)S(1)}, f32[1,1024]{1,0:T(1,128)}, u32[]{:S(2)}) copy-start(f32[1,1024]{1,0:T(1,128)} %get-tuple-element.100) | copy-start | bytes 12292
  402.4 22.7 %copy-start.11 = (f32[1,1024]{1,0:T(1,128)S(1)}, f32[1,1024]{1,0:T(1,128)}, u32[]{:S(2)}) copy-start(f32[1,1024]{1,0:T(1,128)} %get-tuple-element.113) | copy-start | bytes 12292
  402.4 22.7 %copy-start.12 = (f32[1,1024]{1,0:T(1,128)S(1)}, f32[1,1024]{1,0:T(1,128)}, u32[]{:S(2)}) copy-start(f32[1,1024]{1,0:T(1,128)} %get-tuple-element.114) | copy-start | bytes 12292
  493.6 12.6 %copy-start.6 = (f32[128,1024]{1,0:T(8,128)S(1)}, f32[128,1024]{1,0:T(8,128)}, u32[]{:S(2)}) copy-start(f32[128,1024]{1,0:T(8,128)} %get-tuple-element.161) | copy-start | bytes 1572868
  493.6 13.3 %copy-start.7 = (f32[128,1024]{1,0:T(8,128)S(1)}, f32[128,1024]{1,0:T(8,128)}, u32[]{:S(2)}) copy-start(f32[128,1024]{1,0:T(8,128)} %get-tuple-element.162) | copy-start | bytes 1572868
